TPU v7x, 32 devices: a whole 2x2x4 slice. The times are simulated.
32 devices in a mesh: dp: 16 (over z, x, core), expert: 2 (over y).
Axes of the slice: x: 2, y: 2, z: 4, core: 2. Of those that a mesh axis runs over, the one named last changes fastest.
Arguments:
- tokens: bfloat16 [2048, 4096], P('dp', 'expert'), may hold values from -6 to 6
- expert_ids: int32 [2048, 8], P('dp'), may hold values from 0 to 31, all different within a row; in each aligned block of 128 rows (0 to 127, 128 to 255, ...) at most 48 rows name the same one
- gate_prob: float32 [2048, 8], P('dp'), may hold values from 0.05 to 1
- w_gate: bfloat16 [32, 1536, 4096], P('dp', 'expert'), may hold values from -0.09375 to 0.09375
- w_up: bfloat16 [32, 1536, 4096], P('dp', 'expert'), may hold values from -0.09375 to 0.09375
- w_down: bfloat16 [32, 1536, 4096], P('dp', 'expert'), may hold values from -0.21875 to 0.21875
Outputs:
- mixed: bfloat16 [2048, 4096], P('dp', 'expert')
Inputs may be any that keep to these rules, and one draw needn't show every extreme that they name: `expert_ids`: within the 128 tokens of one index of dp no expert is named more than 48 times, a bound that some block reaches; a token's 8 experts differ.
All inputs are finite; a program needn't handle non-finite values.
Results may differ from a plain program's by a relative error of at most 0.014.
Values may be sent and summed in bfloat16 or wider, within the bound.
No kernel may reach another device: no remote copies, remote signals or barrier semaphores. Data moves between devices by JAX's collectives and lax.ppermute only.
A program may use at most 128 MiB of HBM per device.

v0:
```python
import jax
import jax.numpy as jnp
from jax import lax
from jax.sharding import PartitionSpec as P

TOP = 8


def on_device(tokens, expert_ids, gate_prob, w_gate, w_up, w_down):
    dp_count = lax.axis_size("dp")
    tok_rows = tokens.shape[0]
    local_experts = w_gate.shape[0]
    experts_all = local_experts * dp_count
    capacity = 3 * tok_rows * TOP // (2 * experts_all)
    flat_ids = expert_ids.reshape(-1)
    pair_count = flat_ids.shape[0]
    onehot = (flat_ids[:, None] == jnp.arange(experts_all, dtype=jnp.int32)[None, :]).astype(
        jnp.int32
    )
    before = jnp.cumsum(onehot, axis=0, dtype=jnp.int32) - onehot
    slot_pos = jnp.sum(before * onehot, axis=1, dtype=jnp.int32)
    flat_slot = flat_ids * capacity + slot_pos
    owner_row = jnp.arange(pair_count, dtype=jnp.int32) // TOP
    source_row = (
        jnp.full((experts_all * capacity,), tok_rows, jnp.int32).at[flat_slot].set(owner_row)
    )
    weights = gate_prob.reshape(-1)
    gathered = lax.all_gather(tokens, "expert", axis=1, tiled=True)
    padded = jnp.concatenate([gathered, jnp.zeros((1, gathered.shape[1]), gathered.dtype)], axis=0)
    arrived = lax.all_to_all(
        padded[source_row].reshape(dp_count, local_experts, capacity, gathered.shape[1]),
        "dp",
        split_axis=0,
        concat_axis=0,
        tiled=True,
    )
    gate_sum = jnp.einsum("sqcd,qfd->sqcf", arrived, w_gate, preferred_element_type=jnp.float32)
    up_sum = jnp.einsum("sqcd,qfd->sqcf", arrived, w_up, preferred_element_type=jnp.float32)
    hidden = (jax.nn.silu(gate_sum) * up_sum).astype(jnp.bfloat16)
    partial_value = jnp.einsum("sqcf,qfd->sqcd", hidden, w_down, preferred_element_type=jnp.float32)
    partial_value = partial_value.astype(jnp.bfloat16)
    returned = lax.all_to_all(partial_value, "dp", split_axis=0, concat_axis=0, tiled=True)
    flat_rows = returned.reshape(experts_all * capacity, returned.shape[3])
    picked = flat_rows[flat_slot].astype(jnp.float32)
    scaled = picked * weights[:, None]
    return lax.psum_scatter(
        jnp.sum(scaled.reshape(tok_rows, TOP, returned.shape[3]), axis=1).astype(jnp.bfloat16),
        "expert",
        scatter_dimension=1,
        tiled=True,
    )


def solution(mesh):
    in_specs = (
        P("dp", "expert"),
        P("dp", None),
        P("dp", None),
        P("dp", "expert", None),
        P("dp", "expert", None),
        P("dp", "expert", None),
    )
    out_specs = P("dp", "expert")
    return jax.shard_map(
        on_device, mesh=mesh, in_specs=in_specs, out_specs=out_specs, check_vma=False
    )
```

profile of v0, /device:TPU:0, one launch (start us, length us, event | category | flops | bytes accessed | tf_op | source)
XLA Modules:
  0.0 717.5 jit_solution(8234993190053368642)
XLA Ops:
  6.5 0.7 all-gather.2.cloned.1.call-update
  7.3 0.8 copy.17
  8.2 0.7 broadcast_multiply_fusion
  8.9 9.0 %reduce-window.6 = s32[32,8,128]{2,1,0:T(8,128)S(1)} reduce-window(s32[32,8,128]{2,1,0:T(8,128)S(1)} %fusion.22, s32[]{:T(128)} %constant.31.clone.1), window={size=1x1x128 pad=0_0x0_0x127_0}, to_apply=%region_0.0 | reduce-window | flops 4161536 | bytes 262148 | tf_op jit(solution)/shard_map/reduce-window
  18.1 0.1 copy.19
  18.3 0.1 copy.16
  18.4 0.1 mul.37
  18.5 0.1 broadcast_add_fusion
  18.7 4.3 scatter_custom_fusion
  23.0 9.9 %all-gather.2.cloned.1.call-done = bf16[128,4096]{1,0:T(8,128)(2,1)} async-done(((bf16[128,2048]{1,0:T(8,128)(2,1)}), bf16[128,4096]{1,0:T(8,128)(2,1)}) %all-gather.2.cloned.1.call-update) | async-done | bytes 1048592 | tf_op jit(solution)/shard_map/all_gather | solution.py:28
  32.9 1.3 concatenate.3
  34.3 9.6 %gather_fusion = bf16[1536,4096]{1,0:T(8,128)(2,1)} fusion(bf16[129,4096]{1,0:T(8,128)(2,1)S(1)} %concatenate.3, s32[2048]{0:T(1024)S(1)} %pad_clamp_fusion), kind=kCustom, calls=%fused_computation | custom fusion | bytes 25171968 | tf_op jit(solution)/shard_map/gather | solution.py:31
  43.9 277.8 %all_to_all.10 = bf16[16,2,48,4096]{3,2,1,0:T(8,128)(2,1)} all-to-all(bf16[16,2,48,4096]{3,2,1,0:T(8,128)(2,1)} %bitcast.64), channel_id=1, replica_groups=mesh['dp'=16,'expert'=2] {'dp'}, dimensions={0} | all-to-all | bytes 25165824 | tf_op jit(solution)/shard_map/all_to_all | solution.py:30
  321.6 17.9 %fusion.3 = f32[2,16,48,768]{3,2,1,0:T(8,128)} fusion(bf16[2,768,4096]{2,1,0:T(8,128)(2,1)} %param.10, bf16[16,2,48,4096]{3,2,1,0:T(8,128)(2,1)} %all_to_all.10), kind=kOutput, calls=%fused_computation.7 | convolution fusion | flops 9663676416 | bytes 29884416 | tf_op jit(solution)/shard_map/sqcd,qfd->sqcf/dot_general | solution.py:38
  339.6 18.1 %fusion.11 = bf16[16,2,48,768]{3,2,0,1:T(8,128)(2,1)} fusion(f32[2,16,48,768]{3,2,1,0:T(8,128)} %fusion.3, bf16[2,768,4096]{2,1,0:T(8,128)(2,1)} %param.9, bf16[16,2,48,4096]{3,2,1,0:T(8,128)(2,1)} %all_to_all.10), kind=kOutput, calls=%fused_computation.15 | convolution fusion | flops 9670754304 | bytes 32243712 | tf_op jit(solution)/shard_map/sqcd,qfd->sqcf/dot_general | solution.py:37
  357.7 15.1 %convert_bitcast_fusion = bf16[16,2,48,4096]{3,2,0,1:T(8,128)(2,1)S(1)} fusion(bf16[16,2,48,768]{3,2,0,1:T(8,128)(2,1)} %fusion.11, bf16[2,768,4096]{2,1,0:T(8,128)(2,1)} %param.11), kind=kOutput, calls=%fused_computation.11 | convolution fusion | flops 9669967872 | bytes 27525120 | tf_op jit(solution)/shard_map/sqcf,qfd->sqcd/dot_general | solution.py:40
  372.8 5.5 copy.23
  378.3 6.3 all-to-all-start.1
  384.5 0.3 reduce-scatter.2.cloned.1.call-start
  384.8 0.1 copy.24
  384.9 223.4 %all-to-all-done.1 = bf16[16,2,48,4096]{3,2,1,0:T(8,128)(2,1)} async-done(((bf16[16,2,48,4096]{3,2,1,0:T(8,128)(2,1)}), bf16[16,2,48,4096]{3,2,1,0:T(8,128)(2,1)}, u32[]{:S(2)}, u32[]{:S(2)}) %all-to-all-start.1) | async-done | bytes 12582944 | tf_op jit(solution)/shard_map/all_to_all | solution.py:42
  608.3 21.3 %gather_fusion.1 = bf16[1024,4096]{1,0:T(8,128)(2,1)} fusion(bf16[1536,4096]{1,0:T(8,128)(2,1)} %bitcast.14, s32[1024]{0:T(1024)S(1)} %broadcast_clamp_fusion), kind=kCustom, calls=%fused_computation.1 | custom fusion | bytes 16781312 | tf_op jit(solution)/shard_map/gather | solution.py:44
  629.6 12.9 %fusion = bf16[128,4096]{1,0:T(8,128)(2,1)} fusion(bf16[1024,4096]{1,0:T(8,128)(2,1)} %gather_fusion.1, f32[128,8]{1,0:T(8,128)S(1)} %copy.24), kind=kLoop, calls=%fused_computation.4 | loop fusion | flops 12058624 | bytes 9441280 | tf_op jit(solution)/shard_map/reduce_sum | solution.py:47
  642.5 68.2 %reduce-scatter.2.cloned.1.call-done = bf16[128,2048]{1,0:T(8,128)(2,1)} async-done(((bf16[128,4096]{1,0:T(8,128)(2,1)}), bf16[128,2048]{1,0:T(8,128)(2,1)}) %reduce-scatter.2.cloned.1.call-update) | async-done | bytes 524304 | tf_op jit(solution)/shard_map/reduce_scatter | solution.py:46
  (17 shorter events, 0.5 us)
Async XLA Ops:
  6.5 26.4 %all-gather.2.cloned.1.call-start = ((), (), s32[]{:S(2)}) async-start(), calls=%async_computation.3 | async-start | bytes 1572864 | tf_op jit(solution)/shard_map/all_gather | solution.py:28
  378.3 6.6 copy-start
  378.3 230.0 %all-to-all-start.1 = ((bf16[16,2,48,4096]{3,2,1,0:T(8,128)(2,1)}), bf16[16,2,48,4096]{3,2,1,0:T(8,128)(2,1)}, u32[]{:S(2)}, u32[]{:S(2)}) async-start(bf16[16,2,48,4096]{3,2,1,0:T(8,128)(2,1)} %copy.23), calls=%async_computation.1 | async-start | bytes 25165824 | tf_op jit(solution)/shard_map/all_to_all | solution.py:42
  384.5 326.1 %reduce-scatter.2.cloned.1.call-start = ((), (), s32[]{:S(2)}) async-start(), calls=%async_computation.4 | async-start | bytes 1572864 | tf_op jit(solution)/shard_map/reduce_scatter | solution.py:46
Sparse Core Ops, SparseCore 0:
  8.9 23.9 all-gather.1
  642.6 68.0 reduce-scatter.1
where the time goes:
time: 718 us
  waiting for transfers between devices  302 us (42%)
  blocking collectives  278 us (39%)
  matrix products  51.1 us (7%)
  local copies, waits for them, and re-layouts  43.5 us (6%)
  other arithmetic  22.8 us (3%)
  between operations  13.5 us (2%)
    all_to_all x1, blocking collectives, on_device(): lax.all_to_all(padded[source_row].reshape(dp_count, local_experts, capaci...  278 us
    all_to_all x1, waiting for transfers between devices, on_device(): lax.all_to_all(partial_value, 'dp', split_axis=0, concat_axis=0, tiled=True)  223 us
    reduce_scatter x1, waiting for transfers between devices, on_device(): lax.psum_scatter(jnp.sum(scaled.reshape(tok_rows, TOP, returned.shape[3])...  68.2 us
    gather x1, local copies, waits for them, and re-layouts, on_device(): picked = flat_rows[flat_slot].astype(jnp.float32)  21.3 us
    dot_general x1, matrix products, on_device(): jnp.einsum('sqcd,qfd->sqcf', arrived, w_gate, preferred_element_type=jnp....  18.1 us
    dot_general x1, matrix products, on_device(): jnp.einsum('sqcd,qfd->sqcf', arrived, w_up, preferred_element_type=jnp.fl...  17.9 us
    dot_general x1, matrix products, on_device(): jnp.einsum('sqcf,qfd->sqcd', hidden, w_down, preferred_element_type=jnp.f...  15.1 us
  transfers between devices with their start and end apart: 3, of which 3 were waited for; matrix products, arithmetic and copies ran while one was open for 2% of the time, Pallas kernels for 0%

commit v1 on v0

--- a/solution.py
+++ b/solution.py
@@ -1,9 +1,204 @@
+import functools
+
 import jax
 import jax.numpy as jnp
 from jax import lax
+from jax.experimental import pallas as pl
+from jax.experimental.pallas import tpu as pltpu
 from jax.sharding import PartitionSpec as P
 
 TOP = 8
+AXES = ("dp", "expert")
+F32, BF16 = jnp.float32, jnp.bfloat16
+
+BIT = {"Z": 8, "z": 4, "a": 2, "b": 1}
+HOP = {8: "Z", 4: "z", 12: "z", 2: "a", 10: "a", 6: "a", 14: "a", 1: "b", 9: "b", 5: "b", 13: "b", 3: "b", 11: "b", 7: "z", 15: "z"}
+SPREAD = (8, 4, 1, 2, 3, 5, 6, 9, 10, 12, 11, 7, 13, 14, 15)
+
+
+def link_pairs(link):
+    pairs = []
+    for here in range(32):
+        along_x, along_y = 4, 1
+        first = (here >> 1) & 1 == 0
+        step = {"Z": 16, "z": 8, "core": 2, "a": along_x if first else along_y, "b": along_y if first else along_x}[link]
+        pairs.append((here, here ^ step))
+    return pairs
+
+
+def hop(value, link):
+    return lax.ppermute(value, AXES, link_pairs(link))
+
+
+def silu(v):
+    return v / (1.0 + jnp.exp(-v))
+
+
+def experts_kernel(slots, hid_steps, place, *refs):
+    (pieces, (pos, weight, w_gate, w_up, w_down, mine, other, routed, hidden, pick, put, scale)) = refs[:8], refs[8:]
+    step = pl.program_id(0)
+    core, side = place[0], place[1]
+    experts = w_down.shape[0]
+    rows, half = pieces[0].shape
+    used = 4 * slots
+    hid_block = w_gate.shape[1]
+    per_expert = hid_steps // experts
+
+    @pl.when(step == 0)
+    def _():
+        for block in range(4):
+            for e in range(experts):
+                line = block * experts + e
+                at = pl.ds(e * slots, slots)
+                slot = lax.broadcasted_iota(jnp.int32, (slots, rows), 0).astype(F32)
+                chosen = jnp.where(slot == pos[line : line + 1, :], 1.0, 0.0)
+                pick[block, at, :] = chosen.astype(BF16)
+                scale[e, pl.ds(block * slots, slots), :] = jnp.sum(chosen * weight[line : line + 1, :], axis=1, keepdims=True)
+            put[block] = pick[block].astype(F32).T.astype(BF16)
+        for number, piece in enumerate(pieces):
+            own = number < 4
+            a, b = (number % 4) // 2, number % 2
+            first = (core == 0) if own else (core == 1)
+            x, y = jnp.where(first, a, b), jnp.where(first, b, a)
+            block = x + (0 if own else 2)
+            column = (y ^ side) * half
+            chosen = pick[block]
+            row = pl.multiple_of(block * slots, 16)
+            for part in range(4):
+                width = half // 4
+                got = jnp.dot(chosen, piece[:, part * width : (part + 1) * width], preferred_element_type=F32).astype(BF16)
+                to = pl.ds(pl.multiple_of(column + part * width, width), width)
+                for e in range(experts):
+                    routed[e, pl.ds(row, slots), to] = got[e * slots : (e + 1) * slots]
+
+    @pl.when(step < hid_steps)
+    def _():
+        e = step // per_expert
+        at = pl.multiple_of((step % per_expert) * hid_block, hid_block)
+        contract = (((1,), (1,)), ((), ()))
+        rows_in = routed[e]
+        gate = lax.dot_general(rows_in, w_gate[0], contract, preferred_element_type=F32)
+        up = lax.dot_general(rows_in, w_up[0], contract, preferred_element_type=F32)
+        hidden[e, :, pl.ds(at, hid_block)] = (silu(gate) * up).astype(BF16)
+
+    @pl.when(step >= hid_steps)
+    def _():
+        outs = []
+        for e in range(experts):
+            part = jnp.dot(hidden[e], w_down[e], preferred_element_type=F32)
+            outs.append((part * scale[e]).astype(BF16))
+        for block in range(4):
+            these = jnp.concatenate([o[block * slots : (block + 1) * slots] for o in outs], axis=0)
+            total = jnp.dot(put[block], these, preferred_element_type=F32).astype(BF16)
+            if block < 2:
+                mine[block, 0] = total
+            else:
+                other[block - 2, 0] = total
+
+
+def run_experts(place, pieces, pos, weight, w_gate, w_up, w_down, slots):
+    experts, hid, width = w_gate.shape
+    rows, half = pieces[0].shape
+    hid_block, col_block = 256, 512
+    per_expert = hid // hid_block
+    hid_steps, col_steps = experts * per_expert, width // col_block
+    half_steps = half // col_block
+    whole = pl.BlockSpec((rows, half), lambda s, place: (0, 0))
+    small = pl.BlockSpec((4 * experts, rows), lambda s, place: (0, 0))
+
+    def hid_at(s, place):
+        t = jnp.minimum(s, hid_steps - 1)
+        return t // per_expert, t % per_expert, 0
+
+    def col_at(s, place):
+        return 0, 0, jnp.maximum(s - hid_steps, 0)
+
+    def out_at(s, place):
+        t = jnp.maximum(s - hid_steps, 0)
+        return 0, (t // half_steps) ^ place[1], 0, t % half_steps
+
+    used = 4 * slots
+    out = jax.ShapeDtypeStruct((2, 2, rows, half), BF16)
+    return pl.pallas_call(
+        functools.partial(experts_kernel, slots, hid_steps),
+        out_shape=(out, out),
+        grid_spec=pltpu.PrefetchScalarGridSpec(
+            num_scalar_prefetch=1,
+            grid=(hid_steps + col_steps,),
+            in_specs=[whole] * 8
+            + [small, small]
+            + [pl.BlockSpec((1, hid_block, width), hid_at)] * 2
+            + [pl.BlockSpec((experts, hid, col_block), col_at)],
+            out_specs=[pl.BlockSpec((2, 1, rows, col_block), out_at)] * 2,
+            scratch_shapes=[
+                pltpu.VMEM((experts, used, width), BF16),
+                pltpu.VMEM((experts, used, hid), BF16),
+                pltpu.VMEM((4, experts * slots, rows), BF16),
+                pltpu.VMEM((4, rows, experts * slots), BF16),
+                pltpu.VMEM((experts, used, 1), F32),
+            ],
+        ),
+        compiler_params=pltpu.CompilerParams(vmem_limit_bytes=40 << 20),
+        cost_estimate=pl.CostEstimate(
+            flops=6 * experts * used * hid * width,
+            bytes_accessed=6 * experts * hid * width + 32 * rows * half,
+            transcendentals=experts * used * hid,
+        ),
+        name="experts",
+    )(place, *pieces, pos, weight, w_gate, w_up, w_down)
+
+
+def slot_tables(expert_ids, gate_prob, experts_all):
+    named = expert_ids[:, :, None] == jnp.arange(experts_all, dtype=jnp.int32)[None, None, :]
+    chosen = jnp.any(named, axis=1)
+    weight = jnp.sum(jnp.where(named, gate_prob[:, :, None], 0.0), axis=1)
+    rows = expert_ids.shape[0]
+    earlier = jnp.tril(jnp.ones((rows, rows), BF16), -1)
+    before = jnp.dot(earlier, chosen.astype(BF16), preferred_element_type=F32)
+    slot = jnp.where(chosen, before, -1.0)
+    return jnp.stack([slot.T, weight.T], axis=1)
+
+
+def on_block(tokens, expert_ids, gate_prob, w_gate, w_up, w_down):
+    dp_count, me = lax.axis_size("dp"), lax.axis_index("dp")
+    rows, half = tokens.shape
+    experts = w_gate.shape[0]
+    experts_all = experts * dp_count
+    capacity = 3 * rows * TOP // (2 * experts_all)
+    slots = -(-capacity // 16) * 16
+    core = me % 2
+    place = jnp.stack([core, lax.axis_index("expert")]).astype(jnp.int32)
+
+    tables = slot_tables(expert_ids, gate_prob, experts_all)
+    tables = lax.all_to_all(
+        tables.reshape(dp_count, experts, 2, rows), "dp", split_axis=0, concat_axis=0, tiled=True
+    )
+    tables = tables[me ^ jnp.arange(dp_count, dtype=jnp.int32)]
+
+    held = {0: tokens}
+    for j in SPREAD:
+        held[j] = hop(held[j & ~BIT[HOP[j]]], HOP[j])
+    across = {j: hop(held[j], "core") for j in (0, *SPREAD)}
+
+    sums = {}
+    for group in (0, 4, 8, 12):
+        order = [group | b for b in (0, 2, 1, 3)]
+        chosen = jnp.stack([tables[r] for r in order])
+        pos = chosen[:, :, 0].reshape(4 * experts, rows)
+        weight = chosen[:, :, 1].reshape(4 * experts, rows)
+        pieces = [held[group | q] for q in range(4)] + [across[group | q] for q in range(4)]
+        mine, other = run_experts(place, pieces, pos, weight, w_gate, w_up, w_down, slots)
+        back = hop(other, "core")
+        mine, back = (v.reshape(4, rows, half) for v in (mine, back))
+        for q in range(4):
+            at = jnp.where(core == 0, q, (q % 2) * 2 + q // 2)
+            sums[group | q] = [lax.dynamic_index_in_dim(v, at, 0, keepdims=False) for v in (mine, back)]
+
+    def total(j):
+        terms = sums[j] + [hop(total(k), HOP[k]) for k in SPREAD if k & ~BIT[HOP[k]] == j]
+        return sum(t.astype(F32) for t in terms).astype(BF16)
+
+    return total(0)
 
 
 def on_device(tokens, expert_ids, gate_prob, w_gate, w_up, w_down):
@@ -61,6 +256,5 @@
         P("dp", "expert", None),
     )
     out_specs = P("dp", "expert")
-    return jax.shard_map(
-        on_device, mesh=mesh, in_specs=in_specs, out_specs=out_specs, check_vma=False
-    )
+    plan = on_block if (mesh.shape["dp"], mesh.shape["expert"]) == (16, 2) else on_device
+    return jax.shard_map(plan, mesh=mesh, in_specs=in_specs, out_specs=out_specs, check_vma=False)

time: 718 us -> 293 us (0.41)
  blocking collectives: 278 us -> 0 us
  waiting for transfers between devices: 302 us -> 125 us
  Pallas kernels: 0 us -> 104 us
  matrix products: 51.1 us -> 0.2 us
  local copies, waits for them, and re-layouts: 43.5 us -> 6.76 us
  starting transfers between devices: 6.55 us -> 34.9 us
  between operations: 13.5 us -> 0.32 us
    all_to_all x1 -> x0, blocking collectives: 278 us -> none  [on_device(): lax.all_to_all(padded[source_row].reshape(dp_count, local_experts, capaci...]
    all_to_all x1, waiting for transfers between devices: 223 us -> 8.32 us  [on_block(): lax.all_to_all(tables.reshape(dp_count, experts, 2, rows), 'dp', split_ax...]
    ppermute x0 -> x50, waiting for transfers between devices: none -> 116 us  [hop(): return lax.ppermute(value, AXES, link_pairs(link))]
    pallas_call x0 -> x4, Pallas kernels: none -> 104 us  [run_experts(): pl.pallas_call(functools.partial(experts_kernel, slots, hid_steps), out_s...]
    reduce_scatter x1 -> x0, waiting for transfers between devices: 68.2 us -> none  [on_device(): lax.psum_scatter(jnp.sum(scaled.reshape(tok_rows, TOP, returned.shape[3])...]
    dot_general x3 -> x1, matrix products: 51.1 us -> 0.2 us  [slot_tables(): before = jnp.dot(earlier, chosen.astype(BF16), preferred_element_type=F32)]
    ppermute x0 -> x50, starting transfers between devices: none -> 30.3 us  [hop(): return lax.ppermute(value, AXES, link_pairs(link))]
    gather x2 -> x1, local copies, waits for them, and re-layouts: 30.9 us -> 0.59 us  [on_block(): tables = tables[me ^ jnp.arange(dp_count, dtype=jnp.int32)]]
  transfers between devices with their start and end apart: 3 -> 51, of which waited for: 3 -> 14; matrix products, arithmetic and copies ran while one was open for 2% -> 7% of each run, Pallas kernels for 0% -> 36%
where the time goes in v1:
time: 293 us; the launch traced here: 292 us
  waiting for transfers between devices  125 us (43%)
  Pallas kernels  104 us (35%)
  starting transfers between devices  34.9 us (12%)
  other arithmetic  20.5 us (7%)
  local copies, waits for them, and re-layouts  6.76 us (2%)
    ppermute x50, waiting for transfers between devices, hop(): return lax.ppermute(value, AXES, link_pairs(link))  116 us
    pallas_call x4, Pallas kernels, run_experts(): pl.pallas_call(functools.partial(experts_kernel, slots, hid_steps), out_s...  104 us
    ppermute x50, starting transfers between devices, hop(): return lax.ppermute(value, AXES, link_pairs(link))  30.3 us
    convert_element_type x12, other arithmetic, total(): return sum((t.astype(F32) for t in terms)).astype(BF16)  18.3 us
    all_to_all x1, waiting for transfers between devices, on_block(): lax.all_to_all(tables.reshape(dp_count, experts, 2, rows), 'dp', split_ax...  8.32 us
    unnamed x22, local copies, waits for them, and re-layouts  6.13 us
  transfers between devices with their start and end apart: 51, of which 14 were waited for; matrix products, arithmetic and copies ran while one was open for 7% of the time, Pallas kernels for 36%

profile of v1, /device:TPU:0, one launch (start us, length us, event | category | flops | bytes accessed | tf_op | source)
XLA Modules:
  0.0 291.5 jit_solution(8611297889663241424)
XLA Ops:
  0.0 4.0 %collective-permute-start.8 = (bf16[128,2048]{1,0:T(8,128)(2,1)}, bf16[128,2048]{1,0:T(8,128)(2,1)S(1)}, u32[]{:S(2)}, u32[]{:S(2)}) collective-permute-start(bf16[128,2048]{1,0:T(8,128)(2,1)} %refs_0_.1), channel_id=1, source_target_pairs={{0,16},{1,17},{2,18},{3,19},{4,20},{5,21},{6,22},{7,23},{8,24},{9,... | collective-permute-start | bytes 1572872 | tf_op jit(solution)/shard_map/ppermute | solution.py:30
  9.5 18.0 %collective-permute-done.8.refs_0_ = bf16[128,2048]{1,0:T(8,128)(2,1)S(1)} collective-permute-done((bf16[128,2048]{1,0:T(8,128)(2,1)}, bf16[128,2048]{1,0:T(8,128)(2,1)S(1)}, u32[]{:S(2)}, u32[]{:S(2)}) %collective-permute-start.8) | collective-permute-done | bytes 524320 | tf_op jit(solution)/shard_map/ppermute | solution.py:30
  32.6 4.7 %all-to-all-start = ((f32[16,2,2,128]{3,2,1,0:T(2,128)}), f32[16,2,2,128]{3,2,1,0:T(2,128)S(1)}, u32[]{:S(2)}, u32[]{:S(2)}) async-start(f32[16,2,2,128]{3,2,1,0:T(2,128)} %pad_maximum_fusion), calls=%async_computation | async-start | bytes 65536 | tf_op jit(solution)/shard_map/all_to_all | solution.py:173
  37.4 8.3 %all-to-all-done = f32[16,2,2,128]{3,2,1,0:T(2,128)S(1)} async-done(((f32[16,2,2,128]{3,2,1,0:T(2,128)}), f32[16,2,2,128]{3,2,1,0:T(2,128)S(1)}, u32[]{:S(2)}, u32[]{:S(2)}) %all-to-all-start) | async-done | bytes 32800 | tf_op jit(solution)/shard_map/all_to_all | solution.py:173
  49.5 16.7 %collective-permute-done.2.refs_3_ = bf16[128,2048]{1,0:T(8,128)(2,1)S(1)} collective-permute-done((bf16[128,2048]{1,0:T(8,128)(2,1)S(1)}, bf16[128,2048]{1,0:T(8,128)(2,1)S(1)}, u32[]{:S(2)}, u32[]{:S(2)}) %collective-permute-start.2) | collective-permute-done | bytes 524320 | tf_op jit(solution)/shard_map/ppermute | solution.py:30
  67.9 5.5 %collective-permute-done.11.refs_3_ = bf16[128,2048]{1,0:T(8,128)(2,1)S(1)} collective-permute-done((bf16[128,2048]{1,0:T(8,128)(2,1)S(1)}, bf16[128,2048]{1,0:T(8,128)(2,1)S(1)}, u32[]{:S(2)}, u32[]{:S(2)}) %collective-permute-start.11) | collective-permute-done | bytes 524320 | tf_op jit(solution)/shard_map/ppermute | solution.py:30
  74.2 8.9 %collective-permute-done.19.refs_1_ = bf16[128,2048]{1,0:T(8,128)(2,1)S(1)} collective-permute-done((bf16[128,2048]{1,0:T(8,128)(2,1)S(1)}, bf16[128,2048]{1,0:T(8,128)(2,1)S(1)}, u32[]{:S(2)}, u32[]{:S(2)}) %collective-permute-start.19) | collective-permute-done | bytes 524320 | tf_op jit(solution)/shard_map/ppermute | solution.py:30
  84.2 3.2 %collective-permute-done.21.refs_3_ = bf16[128,2048]{1,0:T(8,128)(2,1)S(1)} collective-permute-done((bf16[128,2048]{1,0:T(8,128)(2,1)S(1)}, bf16[128,2048]{1,0:T(8,128)(2,1)S(1)}, u32[]{:S(2)}, u32[]{:S(2)}) %collective-permute-start.21) | collective-permute-done | bytes 524320 | tf_op jit(solution)/shard_map/ppermute | solution.py:30
  88.5 26.6 %experts.4 = (bf16[2,2,128,2048]{3,2,1,0:T(8,128)(2,1)S(1)}, bf16[2,2,128,2048]{3,2,1,0:T(8,128)(2,1)}) custom-call(s32[2]{0:T(128)S(1)} %pad_add_fusion.place, bf16[128,2048]{1,0:T(8,128)(2,1)S(1)} %copy-done.6, bf16[128,2048]{1,0:T(8,128)(2,1)S(1)} %collective-permute-done.refs_1_, bf16[128,2048]{1,0:T(8,128)(2,1)S(1)} %collective-permute-done.1.refs_2_, ...), custom_call_target="tpu_custom_call" | custom-call | flops 7247757312 | bytes 46137344 | tf_op jit(solution)/shard_map/experts/pallas_call | solution.py:122
  119.0 25.3 %experts.6 = (bf16[2,2,128,2048]{3,2,1,0:T(8,128)(2,1)S(1)}, bf16[2,2,128,2048]{3,2,1,0:T(8,128)(2,1)}) custom-call(s32[2]{0:T(128)S(1)} %pad_add_fusion.place, bf16[128,2048]{1,0:T(8,128)(2,1)S(1)} %copy-done.10, bf16[128,2048]{1,0:T(8,128)(2,1)S(1)} %collective-permute-done.19.refs_1_, bf16[128,2048]{1,0:T(8,128)(2,1)S(1)} %collective-permute-done.20.refs_2_, ...), custom_call_target="tpu_custom_call" | custom-call | flops 7247757312 | bytes 46137344 | tf_op jit(solution)/shard_map/experts/pallas_call | solution.py:122
  145.5 26.6 %experts.7 = (bf16[2,2,128,2048]{3,2,1,0:T(8,128)(2,1)S(1)}, bf16[2,2,128,2048]{3,2,1,0:T(8,128)(2,1)}) custom-call(s32[2]{0:T(128)S(1)} %pad_add_fusion.place, bf16[128,2048]{1,0:T(8,128)(2,1)} %collective-permute-done.34.refs_0_, bf16[128,2048]{1,0:T(8,128)(2,1)S(1)} %collective-permute-done.35.refs_1_, ...), custom_call_target="tpu_custom_call" | custom-call | flops 7247757312 | bytes 46137344 | tf_op jit(solution)/shard_map/experts/pallas_call | solution.py:122
  173.9 25.5 %experts.5 = (bf16[2,2,128,2048]{3,2,1,0:T(8,128)(2,1)S(1)}, bf16[2,2,128,2048]{3,2,1,0:T(8,128)(2,1)}) custom-call(s32[2]{0:T(128)S(1)} %pad_add_fusion.place, bf16[128,2048]{1,0:T(8,128)(2,1)S(1)} %collective-permute-done.8.refs_0_, bf16[128,2048]{1,0:T(8,128)(2,1)S(1)} %copy-done.8, bf16[128,2048]{1,0:T(8,128)(2,1)S(1)} %collective-permute-done.10.refs_2_, ...), custom_call_target="tpu_custom_call" | custom-call | flops 7247757312 | bytes 46137344 | tf_op jit(solution)/shard_map/experts/pallas_call | solution.py:122
  202.2 2.1 fusion.16
  205.1 2.1 fusion.19
  211.9 7.2 %collective-permute-done.27 = bf16[128,2048]{1,0:T(8,128)(2,1)S(1)} collective-permute-done((bf16[128,2048]{1,0:T(8,128)(2,1)S(1)}, bf16[128,2048]{1,0:T(8,128)(2,1)S(1)}, u32[]{:S(2)}, u32[]{:S(2)}) %collective-permute-start.27) | collective-permute-done | bytes 524320 | tf_op jit(solution)/shard_map/ppermute | solution.py:30
  220.4 9.5 %collective-permute-done.47 = bf16[128,2048]{1,0:T(8,128)(2,1)S(1)} collective-permute-done((bf16[128,2048]{1,0:T(8,128)(2,1)S(1)}, bf16[128,2048]{1,0:T(8,128)(2,1)S(1)}, u32[]{:S(2)}, u32[]{:S(2)}) %collective-permute-start.47) | collective-permute-done | bytes 524320 | tf_op jit(solution)/shard_map/ppermute | solution.py:30
  231.2 2.1 collective-permute-start.43
  234.6 8.4 %collective-permute-done.28 = bf16[128,2048]{1,0:T(8,128)(2,1)S(1)} collective-permute-done((bf16[128,2048]{1,0:T(8,128)(2,1)S(1)}, bf16[128,2048]{1,0:T(8,128)(2,1)S(1)}, u32[]{:S(2)}, u32[]{:S(2)}) %collective-permute-start.28) | collective-permute-done | bytes 524320 | tf_op jit(solution)/shard_map/ppermute | solution.py:30
  244.4 5.9 %collective-permute-done.43 = bf16[128,2048]{1,0:T(8,128)(2,1)S(1)} collective-permute-done((bf16[128,2048]{1,0:T(8,128)(2,1)S(1)}, bf16[128,2048]{1,0:T(8,128)(2,1)S(1)}, u32[]{:S(2)}, u32[]{:S(2)}) %collective-permute-start.43) | collective-permute-done | bytes 524320 | tf_op jit(solution)/shard_map/ppermute | solution.py:30
  252.3 7.3 %collective-permute-done.48 = bf16[128,2048]{1,0:T(8,128)(2,1)S(1)} collective-permute-done((bf16[128,2048]{1,0:T(8,128)(2,1)S(1)}, bf16[128,2048]{1,0:T(8,128)(2,1)S(1)}, u32[]{:S(2)}, u32[]{:S(2)}) %collective-permute-start.48) | collective-permute-done | bytes 524320 | tf_op jit(solution)/shard_map/ppermute | solution.py:30
  261.1 4.1 %collective-permute-done.32 = bf16[128,2048]{1,0:T(8,128)(2,1)S(1)} collective-permute-done((bf16[128,2048]{1,0:T(8,128)(2,1)S(1)}, bf16[128,2048]{1,0:T(8,128)(2,1)S(1)}, u32[]{:S(2)}, u32[]{:S(2)}) %collective-permute-start.32) | collective-permute-done | bytes 524320 | tf_op jit(solution)/shard_map/ppermute | solution.py:30
  267.6 14.4 %collective-permute-done.45 = bf16[128,2048]{1,0:T(8,128)(2,1)S(1)} collective-permute-done((bf16[128,2048]{1,0:T(8,128)(2,1)S(1)}, bf16[128,2048]{1,0:T(8,128)(2,1)S(1)}, u32[]{:S(2)}, u32[]{:S(2)}) %collective-permute-start.45) | collective-permute-done | bytes 524320 | tf_op jit(solution)/shard_map/ppermute | solution.py:30
  282.0 7.2 %collective-permute-done.33 = bf16[128,2048]{1,0:T(8,128)(2,1)S(1)} collective-permute-done((bf16[128,2048]{1,0:T(8,128)(2,1)S(1)}, bf16[128,2048]{1,0:T(8,128)(2,1)S(1)}, u32[]{:S(2)}, u32[]{:S(2)}) %collective-permute-start.33) | collective-permute-done | bytes 524320 | tf_op jit(solution)/shard_map/ppermute | solution.py:30
  289.2 2.3 fusion.14
  (132 shorter events, 45.2 us)
Async XLA Ops:
  0.0 27.5 %collective-permute-start.8 = (bf16[128,2048]{1,0:T(8,128)(2,1)}, bf16[128,2048]{1,0:T(8,128)(2,1)S(1)}, u32[]{:S(2)}, u32[]{:S(2)}) collective-permute-start(bf16[128,2048]{1,0:T(8,128)(2,1)} %refs_0_.1), channel_id=1, source_target_pairs={{0,16},{1,17},{2,18},{3,19},{4,20},{5,21},{6,22},{7,23},{8,24},{9,... | collective-permute-start | bytes 1572872 | tf_op jit(solution)/shard_map/ppermute | solution.py:30
  4.0 25.0 %collective-permute-start.1 = (bf16[128,2048]{1,0:T(8,128)(2,1)}, bf16[128,2048]{1,0:T(8,128)(2,1)S(1)}, u32[]{:S(2)}, u32[]{:S(2)}) collective-permute-start(bf16[128,2048]{1,0:T(8,128)(2,1)} %refs_0_.1), channel_id=1, source_target_pairs={{0,4},{1,5},{2,3},{3,2},{4,0},{5,1},{6,7},{7,6},{8,12},{9,13},{10,... | collective-permute-start | bytes 1572872 | tf_op jit(solution)/shard_map/ppermute | solution.py:30
  5.5 24.2 %collective-permute-start.34 = (bf16[128,2048]{1,0:T(8,128)(2,1)}, bf16[128,2048]{1,0:T(8,128)(2,1)}, u32[]{:S(2)}, u32[]{:S(2)}) collective-permute-start(bf16[128,2048]{1,0:T(8,128)(2,1)} %refs_0_.1), channel_id=1, source_target_pairs={{0,8},{1,9},{2,10},{3,11},{4,12},{5,13},{6,14},{7,15},{8,0},{9,1},... | collective-permute-start | bytes 1572872 | tf_op jit(solution)/shard_map/ppermute | solution.py:30
  7.1 39.2 %collective-permute-start = (bf16[128,2048]{1,0:T(8,128)(2,1)}, bf16[128,2048]{1,0:T(8,128)(2,1)S(1)}, u32[]{:S(2)}, u32[]{:S(2)}) collective-permute-start(bf16[128,2048]{1,0:T(8,128)(2,1)} %refs_0_.1), channel_id=1, source_target_pairs={{0,1},{1,0},{2,6},{3,7},{4,5},{5,4},{6,2},{7,3},{8,9},{9,8},{10,14... | collective-permute-start | bytes 1572872 | tf_op jit(solution)/shard_map/ppermute | solution.py:30
  8.6 38.3 %collective-permute-start.3 = (bf16[128,2048]{1,0:T(8,128)(2,1)}, bf16[128,2048]{1,0:T(8,128)(2,1)}, u32[]{:S(2)}, u32[]{:S(2)}) collective-permute-start(bf16[128,2048]{1,0:T(8,128)(2,1)} %refs_0_.1), channel_id=1, source_target_pairs={{0,2},{1,3},{2,0},{3,1},{4,6},{5,7},{6,4},{7,5},{8,10},{9,11},{10,... | collective-permute-start | bytes 1572872 | tf_op jit(solution)/shard_map/ppermute | solution.py:30
  48.8 24.6 %collective-permute-start.11 = (bf16[128,2048]{1,0:T(8,128)(2,1)S(1)}, bf16[128,2048]{1,0:T(8,128)(2,1)S(1)}, u32[]{:S(2)}, u32[]{:S(2)}) collective-permute-start(bf16[128,2048]{1,0:T(8,128)(2,1)S(1)} %collective-permute-done.10.refs_2_), channel_id=1, source_target_pairs={{0,1},{1,0},{2,6},{3,7},{4,5},{5,4},{6,2},{7,3},{8,9},{9,8},{10,14... | collective-permute-start | bytes 1572872 | tf_op jit(solution)/shard_map/ppermute | solution.py:30
  74.1 42.3 %collective-permute-start.22 = (bf16[128,2048]{1,0:T(8,128)(2,1)S(1)}, bf16[128,2048]{1,0:T(8,128)(2,1)S(1)}, u32[]{:S(2)}, u32[]{:S(2)}) collective-permute-start(bf16[128,2048]{1,0:T(8,128)(2,1)S(1)} %collective-permute-done.18.refs_0_), channel_id=1, source_target_pairs={{0,2},{1,3},{2,0},{3,1},{4,6},{5,7},{6,4},{7,5},{8,10},{9,11},{10,... | collective-permute-start | bytes 1572872 | tf_op jit(solution)/shard_map/ppermute | solution.py:30
  83.1 33.9 %collective-permute-start.37 = (bf16[128,2048]{1,0:T(8,128)(2,1)S(1)}, bf16[128,2048]{1,0:T(8,128)(2,1)S(1)}, u32[]{:S(2)}, u32[]{:S(2)}) collective-permute-start(bf16[128,2048]{1,0:T(8,128)(2,1)S(1)} %collective-permute-done.2.refs_3_), channel_id=1, source_target_pairs={{0,8},{1,9},{2,10},{3,11},{4,12},{5,13},{6,14},{7,15},{8,0},{9,1},... | collective-permute-start | bytes 1572872 | tf_op jit(solution)/shard_map/ppermute | solution.py:30
  83.7 33.3 %collective-permute-start.23 = (bf16[128,2048]{1,0:T(8,128)(2,1)S(1)}, bf16[128,2048]{1,0:T(8,128)(2,1)S(1)}, u32[]{:S(2)}, u32[]{:S(2)}) collective-permute-start(bf16[128,2048]{1,0:T(8,128)(2,1)S(1)} %collective-permute-done.19.refs_1_), channel_id=1, source_target_pairs={{0,2},{1,3},{2,0},{3,1},{4,6},{5,7},{6,4},{7,5},{8,10},{9,11},{10,... | collective-permute-start | bytes 1572872 | tf_op jit(solution)/shard_map/ppermute | solution.py:30
  83.7 33.8 %collective-permute-start.24 = (bf16[128,2048]{1,0:T(8,128)(2,1)S(1)}, bf16[128,2048]{1,0:T(8,128)(2,1)S(1)}, u32[]{:S(2)}, u32[]{:S(2)}) collective-permute-start(bf16[128,2048]{1,0:T(8,128)(2,1)S(1)} %collective-permute-done.20.refs_2_), channel_id=1, source_target_pairs={{0,2},{1,3},{2,0},{3,1},{4,6},{5,7},{6,4},{7,5},{8,10},{9,11},{10,... | collective-permute-start | bytes 1572872 | tf_op jit(solution)/shard_map/ppermute | solution.py:30
  87.4 30.1 %collective-permute-start.25 = (bf16[128,2048]{1,0:T(8,128)(2,1)S(1)}, bf16[128,2048]{1,0:T(8,128)(2,1)S(1)}, u32[]{:S(2)}, u32[]{:S(2)}) collective-permute-start(bf16[128,2048]{1,0:T(8,128)(2,1)S(1)} %collective-permute-done.21.refs_3_), channel_id=1, source_target_pairs={{0,2},{1,3},{2,0},{3,1},{4,6},{5,7},{6,4},{7,5},{8,10},{9,11},{10,... | collective-permute-start | bytes 1572872 | tf_op jit(solution)/shard_map/ppermute | solution.py:30
  116.4 27.9 %collective-permute-start.12 = (bf16[128,2048]{1,0:T(8,128)(2,1)S(1)}, bf16[128,2048]{1,0:T(8,128)(2,1)S(1)}, u32[]{:S(2)}, u32[]{:S(2)}) collective-permute-start(bf16[128,2048]{1,0:T(8,128)(2,1)S(1)} %collective-permute-done.8.refs_0_), channel_id=1, source_target_pairs={{0,2},{1,3},{2,0},{3,1},{4,6},{5,7},{6,4},{7,5},{8,10},{9,11},{10,... | collective-permute-start | bytes 1572872 | tf_op jit(solution)/shard_map/ppermute | solution.py:30
  117.0 27.5 %collective-permute-start.38 = (bf16[128,2048]{1,0:T(8,128)(2,1)}, bf16[128,2048]{1,0:T(8,128)(2,1)S(1)}, u32[]{:S(2)}, u32[]{:S(2)}) collective-permute-start(bf16[128,2048]{1,0:T(8,128)(2,1)} %collective-permute-done.34.refs_0_), channel_id=1, source_target_pairs={{0,2},{1,3},{2,0},{3,1},{4,6},{5,7},{6,4},{7,5},{8,10},{9,11},{10,... | collective-permute-start | bytes 1572872 | tf_op jit(solution)/shard_map/ppermute | solution.py:30
  117.0 27.8 %collective-permute-start.39 = (bf16[128,2048]{1,0:T(8,128)(2,1)S(1)}, bf16[128,2048]{1,0:T(8,128)(2,1)S(1)}, u32[]{:S(2)}, u32[]{:S(2)}) collective-permute-start(bf16[128,2048]{1,0:T(8,128)(2,1)S(1)} %collective-permute-done.35.refs_1_), channel_id=1, source_target_pairs={{0,2},{1,3},{2,0},{3,1},{4,6},{5,7},{6,4},{7,5},{8,10},{9,11},{10,... | collective-permute-start | bytes 1572872 | tf_op jit(solution)/shard_map/ppermute | solution.py:30
  117.5 27.5 %collective-permute-start.40 = (bf16[128,2048]{1,0:T(8,128)(2,1)S(1)}, bf16[128,2048]{1,0:T(8,128)(2,1)S(1)}, u32[]{:S(2)}, u32[]{:S(2)}) collective-permute-start(bf16[128,2048]{1,0:T(8,128)(2,1)S(1)} %collective-permute-done.36.refs_2_), channel_id=1, source_target_pairs={{0,2},{1,3},{2,0},{3,1},{4,6},{5,7},{6,4},{7,5},{8,10},{9,11},{10,... | collective-permute-start | bytes 1572872 | tf_op jit(solution)/shard_map/ppermute | solution.py:30
  117.5 27.8 %collective-permute-start.41 = (bf16[128,2048]{1,0:T(8,128)(2,1)S(1)}, bf16[128,2048]{1,0:T(8,128)(2,1)S(1)}, u32[]{:S(2)}, u32[]{:S(2)}) collective-permute-start(bf16[128,2048]{1,0:T(8,128)(2,1)S(1)} %collective-permute-done.37.refs_3_), channel_id=1, source_target_pairs={{0,2},{1,3},{2,0},{3,1},{4,6},{5,7},{6,4},{7,5},{8,10},{9,11},{10,... | collective-permute-start | bytes 1572872 | tf_op jit(solution)/shard_map/ppermute | solution.py:30
  144.3 29.1 %collective-permute-start.14 = (bf16[128,2048]{1,0:T(8,128)(2,1)S(1)}, bf16[128,2048]{1,0:T(8,128)(2,1)S(1)}, u32[]{:S(2)}, u32[]{:S(2)}) collective-permute-start(bf16[128,2048]{1,0:T(8,128)(2,1)S(1)} %collective-permute-done.10.refs_2_), channel_id=1, source_target_pairs={{0,2},{1,3},{2,0},{3,1},{4,6},{5,7},{6,4},{7,5},{8,10},{9,11},{10,... | collective-permute-start | bytes 1572872 | tf_op jit(solution)/shard_map/ppermute | solution.py:30
  144.4 29.4 %collective-permute-start.13 = (bf16[128,2048]{1,0:T(8,128)(2,1)S(1)}, bf16[128,2048]{1,0:T(8,128)(2,1)S(1)}, u32[]{:S(2)}, u32[]{:S(2)}) collective-permute-start(bf16[128,2048]{1,0:T(8,128)(2,1)S(1)} %copy-done.8), channel_id=1, source_target_pairs={{0,2},{1,3},{2,0},{3,1},{4,6},{5,7},{6,4},{7,5},{8,10},{9,11},{10,... | collective-permute-start | bytes 1572872 | tf_op jit(solution)/shard_map/ppermute | solution.py:30
  144.9 55.9 %collective-permute-start.7 = (bf16[2,2,128,2048]{3,2,1,0:T(8,128)(2,1)}, bf16[2,2,128,2048]{3,2,1,0:T(8,128)(2,1)}, u32[]{:S(2)}, u32[]{:S(2)}) collective-permute-start(bf16[2,2,128,2048]{3,2,1,0:T(8,128)(2,1)} %get-tuple-element.14), channel_id=1, source_target_pairs={{0,2},{1,3},{2,0},{3,1},{4,6},{5,7},{6,4},{7,5},{8,10},{9,11},{10,... | collective-permute-start | bytes 6291464 | tf_op jit(solution)/shard_map/ppermute | solution.py:30
  144.9 28.9 %collective-permute-start.15 = (bf16[128,2048]{1,0:T(8,128)(2,1)S(1)}, bf16[128,2048]{1,0:T(8,128)(2,1)S(1)}, u32[]{:S(2)}, u32[]{:S(2)}) collective-permute-start(bf16[128,2048]{1,0:T(8,128)(2,1)S(1)} %collective-permute-done.11.refs_3_), channel_id=1, source_target_pairs={{0,2},{1,3},{2,0},{3,1},{4,6},{5,7},{6,4},{7,5},{8,10},{9,11},{10,... | collective-permute-start | bytes 1572872 | tf_op jit(solution)/shard_map/ppermute | solution.py:30
  145.4 56.8 %collective-permute-start.26 = (bf16[2,2,128,2048]{3,2,1,0:T(8,128)(2,1)}, bf16[2,2,128,2048]{3,2,1,0:T(8,128)(2,1)}, u32[]{:S(2)}, u32[]{:S(2)}) collective-permute-start(bf16[2,2,128,2048]{3,2,1,0:T(8,128)(2,1)} %get-tuple-element.18), channel_id=1, source_target_pairs={{0,2},{1,3},{2,0},{3,1},{4,6},{5,7},{6,4},{7,5},{8,10},{9,11},{10,... | collective-permute-start | bytes 6291464 | tf_op jit(solution)/shard_map/ppermute | solution.py:30
  173.4 31.6 %collective-permute-start.42 = (bf16[2,2,128,2048]{3,2,1,0:T(8,128)(2,1)}, bf16[2,2,128,2048]{3,2,1,0:T(8,128)(2,1)}, u32[]{:S(2)}, u32[]{:S(2)}) collective-permute-start(bf16[2,2,128,2048]{3,2,1,0:T(8,128)(2,1)} %get-tuple-element.20), channel_id=1, source_target_pairs={{0,2},{1,3},{2,0},{3,1},{4,6},{5,7},{6,4},{7,5},{8,10},{9,11},{10,... | collective-permute-start | bytes 6291464 | tf_op jit(solution)/shard_map/ppermute | solution.py:30
  202.1 65.5 %collective-permute-start.46 = (bf16[128,2048]{1,0:T(8,128)(2,1)S(1)}, bf16[128,2048]{1,0:T(8,128)(2,1)S(1)}, u32[]{:S(2)}, u32[]{:S(2)}) collective-permute-start(bf16[128,2048]{1,0:T(8,128)(2,1)S(1)} %fusion.21), channel_id=1, source_target_pairs={{0,1},{1,0},{2,6},{3,7},{4,5},{5,4},{6,2},{7,3},{8,9},{9,8},{10,14... | collective-permute-start | bytes 1572872 | tf_op jit(solution)/shard_map/ppermute | solution.py:30
  209.7 51.2 %collective-permute-start.17 = (bf16[128,2048]{1,0:T(8,128)(2,1)S(1)}, bf16[128,2048]{1,0:T(8,128)(2,1)S(1)}, u32[]{:S(2)}, u32[]{:S(2)}) collective-permute-start(bf16[128,2048]{1,0:T(8,128)(2,1)S(1)} %fusion.15), channel_id=1, source_target_pairs={{0,1},{1,0},{2,6},{3,7},{4,5},{5,4},{6,2},{7,3},{8,9},{9,8},{10,14... | collective-permute-start | bytes 1572872 | tf_op jit(solution)/shard_map/ppermute | solution.py:30
  (38 other events, 654.3 us)

commit v2 on v0

--- a/solution.py
+++ b/solution.py
@@ -1,9 +1,381 @@
+import functools
+
 import jax
 import jax.numpy as jnp
 from jax import lax
+from jax.experimental import pallas as pl
+from jax.experimental.pallas import tpu as pltpu
 from jax.sharding import PartitionSpec as P
 
 TOP = 8
+AXES = ("dp", "expert")
+F32, BF16 = jnp.float32, jnp.bfloat16
+
+BIT = {"Z": 8, "z": 4, "a": 2, "b": 1}
+HOP = {8: "Z", 4: "z", 12: "z", 2: "a", 10: "a", 6: "a", 14: "a", 1: "b", 9: "b", 5: "b", 13: "b", 3: "b", 11: "b", 7: "z", 15: "z"}
+SPREAD = (8, 4, 1, 2, 3, 5, 6, 9, 10, 12, 11, 7, 13, 14, 15)
+
+
+def link_pairs(link):
+    pairs = []
+    for here in range(32):
+        along_x, along_y = 4, 1
+        first = (here >> 1) & 1 == 0
+        step = {"Z": 16, "z": 8, "core": 2, "a": along_x if first else along_y, "b": along_y if first else along_x}[link]
+        pairs.append((here, here ^ step))
+    return pairs
+
+
+def hop(value, link):
+    return lax.ppermute(value, AXES, link_pairs(link))
+
+
+def silu(v):
+    return v / (1.0 + jnp.exp(-v))
+
+
+def hidden_kernel(slots, ring, *refs):
+    groups = (len(refs) - 14) // 5
+    count = 8 * groups
+    own, across, refs = refs[: 4 * groups], refs[4 * groups : 5 * groups], refs[5 * groups :]
+    pieces = list(own) + [a.at[q] for a in across for q in range(4)]
+    (pos, w_gate, w_up, out), scratch = refs[:4], refs[4:]
+    held, gates, ups, routed, hidden, pick, piece_sem, gate_sem, up_sem, out_sem = scratch
+    core, side = lax.axis_index("dp") % 2, lax.axis_index("expert")
+    experts, hid, width = w_gate.shape
+    rows, half = pieces[0].shape
+    blocks = count // 2
+    hid_block = gates.shape[1]
+    per_expert = hid // hid_block
+    hid_steps = experts * per_expert
+
+    def piece_copy(i):
+        return pltpu.make_async_copy(pieces[i], held.at[i], piece_sem.at[i])
+
+    def weight_copies(i):
+        at, slot = pl.ds((i % per_expert) * hid_block, hid_block), i % ring
+        return (
+            pltpu.make_async_copy(w_gate.at[i // per_expert, at], gates.at[slot], gate_sem.at[slot]),
+            pltpu.make_async_copy(w_up.at[i // per_expert, at], ups.at[slot], up_sem.at[slot]),
+        )
+
+    for i in range(count):
+        piece_copy(i).start()
+    for i in range(ring):
+        for copy in weight_copies(i):
+            copy.start()
+
+    slot = lax.broadcasted_iota(jnp.int32, (slots, rows), 0).astype(F32)
+    for block in range(blocks):
+        for e in range(experts):
+            line = block * experts + e
+            pick[block, pl.ds(e * slots, slots), :] = jnp.where(slot == pos[line : line + 1, :], 1.0, 0.0).astype(BF16)
+
+    for number in range(count):
+        piece_copy(number).wait()
+        a, b = (number % 4) // 2, number % 2
+        first = (core == 0) if number < blocks else (core == 1)
+        x, y = jnp.where(first, a, b), jnp.where(first, b, a)
+        block = x + 2 * (number // 4)
+        column = (y ^ side) * half
+        chosen = pick[block]
+        row = pl.multiple_of(block * slots, 16)
+        cut = half // 4
+        for part in range(4):
+            got = jnp.dot(chosen, held[number, :, part * cut : (part + 1) * cut], preferred_element_type=F32).astype(BF16)
+            to = pl.ds(pl.multiple_of(column + part * cut, cut), cut)
+            for e in range(experts):
+                routed[e, pl.ds(row, slots), to] = got[e * slots : (e + 1) * slots]
+
+    def hid_step(i, carry):
+        for copy in weight_copies(i):
+            copy.wait()
+        e, slot = i // per_expert, i % ring
+        at = pl.multiple_of((i % per_expert) * hid_block, hid_block)
+        contract = (((1,), (1,)), ((), ()))
+        gate = lax.dot_general(routed[e], gates[slot], contract, preferred_element_type=F32)
+        up = lax.dot_general(routed[e], ups[slot], contract, preferred_element_type=F32)
+        hidden[e, :, pl.ds(at, hid_block)] = (silu(gate) * up).astype(BF16)
+
+        @pl.when(i + ring < hid_steps)
+        def _():
+            for copy in weight_copies(i + ring):
+                copy.start()
+
+        return carry
+
+    lax.fori_loop(0, hid_steps, hid_step, 0)
+    done = pltpu.make_async_copy(hidden, out, out_sem)
+    done.start()
+    done.wait()
+
+
+def output_kernel(slots, groups, *refs):
+    pos, weight, given, w_down, mine = refs[:5]
+    others, scratch = refs[5 : 5 + groups], refs[5 + groups :]
+    hidden, downs, put, scale, stage, given_sem, down_sem, out_sem = scratch
+    side = lax.axis_index("expert")
+    experts, hid, width = w_down.shape
+    _, _, rows, half = mine.shape
+    col_block = downs.shape[3]
+    half_steps = half // col_block
+    col_steps = width // col_block
+    blocks = 4 * groups
+
+    def down_copy(c):
+        at = pl.ds(pl.multiple_of(c * col_block, col_block), col_block)
+        return pltpu.make_async_copy(w_down.at[:, :, at], downs.at[c], down_sem.at[c])
+
+    def out_copies(c):
+        to, slot = (c // half_steps) ^ side, c % 2
+        at = pl.ds(pl.multiple_of((c % half_steps) * col_block, col_block), col_block)
+        copies = [pltpu.make_async_copy(stage.at[slot, pl.ds(0, 2 * groups)], mine.at[:, to, :, at], out_sem.at[slot, 0])]
+        for g, other in enumerate(others):
+            part = stage.at[slot, pl.ds(2 * groups + 2 * g, 2)]
+            copies.append(pltpu.make_async_copy(part, other.at[:, to, :, at], out_sem.at[slot, 1 + g]))
+        return copies
+
+    given_copy = pltpu.make_async_copy(given, hidden, given_sem)
+    given_copy.start()
+    for c in range(col_steps):
+        down_copy(c).start()
+
+    slot = lax.broadcasted_iota(jnp.int32, (slots, rows), 0).astype(F32)
+    for block in range(blocks):
+        picks = []
+        for e in range(experts):
+            line = block * experts + e
+            chosen = jnp.where(slot == pos[line : line + 1, :], 1.0, 0.0)
+            scale[e, pl.ds(block * slots, slots), :] = jnp.sum(chosen * weight[line : line + 1, :], axis=1, keepdims=True)
+            picks.append(chosen)
+        put[block] = jnp.concatenate(picks, axis=0).T.astype(BF16)
+    given_copy.wait()
+
+    def col_step(c, carry):
+        down_copy(c).wait()
+
+        @pl.when(c >= 2)
+        def _():
+            for copy in out_copies(c - 2):
+                copy.wait()
+
+        outs = []
+        for e in range(experts):
+            part = jnp.dot(hidden[e], downs[c, e], preferred_element_type=F32)
+            outs.append((part * scale[e]).astype(BF16))
+        for block in range(blocks):
+            these = jnp.concatenate([o[block * slots : (block + 1) * slots] for o in outs], axis=0)
+            stage[c % 2, block] = jnp.dot(put[block], these, preferred_element_type=F32).astype(BF16)
+        for copy in out_copies(c):
+            copy.start()
+        return carry
+
+    lax.fori_loop(0, col_steps, col_step, 0)
+    for c in (col_steps - 2, col_steps - 1):
+        for copy in out_copies(c):
+            copy.wait()
+
+
+ANYWHERE = pl.BlockSpec(memory_space=pl.ANY)
+IN_VMEM = pl.BlockSpec(memory_space=pltpu.VMEM)
+
+
+def run_hidden(own, across, pos, w_gate, w_up, slots):
+    experts, hid, width = w_gate.shape
+    rows, half = own[0].shape
+    hid_block, ring = 256, 3
+    count = 2 * len(own)
+    blocks = count // 2
+    used = blocks * slots
+    return pl.pallas_call(
+        functools.partial(hidden_kernel, slots, ring),
+        out_shape=jax.ShapeDtypeStruct((experts, used, hid), BF16),
+        in_specs=[ANYWHERE] * (len(own) + len(across)) + [IN_VMEM] + [ANYWHERE] * 2,
+        out_specs=ANYWHERE,
+        scratch_shapes=[
+            pltpu.VMEM((count, rows, half), BF16),
+            pltpu.VMEM((ring, hid_block, width), BF16),
+            pltpu.VMEM((ring, hid_block, width), BF16),
+            pltpu.VMEM((experts, used, width), BF16),
+            pltpu.VMEM((experts, used, hid), BF16),
+            pltpu.VMEM((blocks, experts * slots, rows), BF16),
+            pltpu.SemaphoreType.DMA((count,)),
+            pltpu.SemaphoreType.DMA((ring,)),
+            pltpu.SemaphoreType.DMA((ring,)),
+            pltpu.SemaphoreType.DMA,
+        ],
+        compiler_params=pltpu.CompilerParams(vmem_limit_bytes=48 << 20),
+        cost_estimate=pl.CostEstimate(
+            flops=4 * experts * used * hid * width,
+            bytes_accessed=4 * experts * hid * width + 2 * count * rows * half,
+            transcendentals=experts * used * hid,
+        ),
+        name="hidden_units",
+    )(*own, *across, pos, w_gate, w_up)
+
+
+def run_outputs(hidden, pos, weight, w_down, slots, half):
+    experts, hid, width = w_down.shape
+    lines, rows = pos.shape
+    col_block = 512
+    blocks = lines // experts
+    groups = blocks // 4
+    used = blocks * slots
+    mine = jax.ShapeDtypeStruct((2 * groups, 2, rows, half), BF16)
+    other = jax.ShapeDtypeStruct((2, 2, rows, half), BF16)
+    return pl.pallas_call(
+        functools.partial(output_kernel, slots, groups),
+        out_shape=(mine,) + (other,) * groups,
+        in_specs=[IN_VMEM] * 2 + [ANYWHERE] * 2,
+        out_specs=(ANYWHERE,) * (1 + groups),
+        scratch_shapes=[
+            pltpu.VMEM((experts, used, hid), BF16),
+            pltpu.VMEM((width // col_block, experts, hid, col_block), BF16),
+            pltpu.VMEM((blocks, rows, experts * slots), BF16),
+            pltpu.VMEM((experts, used, 1), F32),
+            pltpu.VMEM((2, blocks, rows, col_block), BF16),
+            pltpu.SemaphoreType.DMA,
+            pltpu.SemaphoreType.DMA((width // col_block,)),
+            pltpu.SemaphoreType.DMA((2, 1 + groups)),
+        ],
+        compiler_params=pltpu.CompilerParams(vmem_limit_bytes=48 << 20),
+        cost_estimate=pl.CostEstimate(
+            flops=2 * experts * used * hid * width,
+            bytes_accessed=2 * experts * hid * width + 4 * blocks * rows * half,
+            transcendentals=0,
+        ),
+        name="weighted_outputs",
+    )(pos, weight, hidden, w_down)
+
+
+def slot_tables(expert_ids, gate_prob, experts_all):
+    named = expert_ids[:, :, None] == jnp.arange(experts_all, dtype=jnp.int32)[None, None, :]
+    chosen = jnp.any(named, axis=1)
+    weight = jnp.sum(jnp.where(named, gate_prob[:, :, None], 0.0), axis=1)
+    rows = expert_ids.shape[0]
+    earlier = jnp.tril(jnp.ones((rows, rows), BF16), -1)
+    before = jnp.dot(earlier, chosen.astype(BF16), preferred_element_type=F32)
+    slot = jnp.where(chosen, before, -1.0)
+    return jnp.stack([slot.T, weight.T], axis=1)
+
+
+SPREAD_AFTER = (
+    (4, ()),
+    (8, ()),
+    (2, ()),
+    (1, ()),
+    (3, ()),
+    ('tables', (1, 2)),
+    (5, (8,)),
+    (6, (8,)),
+    (10, (4,)),
+    (12, ()),
+    (7, (3, 8)),
+    (11, (5,)),
+    (('c', 0), ()),
+    (9, (10, 5)),
+    (('c', 4), ()),
+    (13, (11, 6)),
+    (14, (11, 6)),
+    (15, (7,)),
+)
+
+COLLECT_AFTER = (
+    (15, ()),
+    (13, ()),
+    (14, ()),
+    (9, ()),
+    (11, ()),
+    (12, ()),
+    (7, ()),
+    (5, ()),
+    (6, ()),
+    (10, ()),
+    (8, ()),
+    (1, ()),
+    (3, ()),
+    (4, ()),
+    (2, ()),
+)
+
+
+def after(value, *earlier):
+    return lax.optimization_barrier((value, *earlier))[0] if earlier else value
+
+
+def on_block(tokens, expert_ids, gate_prob, w_gate, w_up, w_down):
+    dp_count, me = lax.axis_size("dp"), lax.axis_index("dp")
+    rows, half = tokens.shape
+    experts = w_gate.shape[0]
+    experts_all = experts * dp_count
+    capacity = 3 * rows * TOP // (2 * experts_all)
+    slots = -(-capacity // 16) * 16
+    core = me % 2
+
+    held = {0: tokens}
+
+    def tables_after(*earlier):
+        own = after(slot_tables(expert_ids, gate_prob, experts_all), *earlier)
+        every = lax.all_to_all(
+            own.reshape(dp_count, experts, 2, rows), "dp", split_axis=0, concat_axis=0, tiled=True
+        )
+        return every[me ^ jnp.arange(dp_count, dtype=jnp.int32)]
+
+    def tables_of(groups):
+        order = [group | b for group in groups for b in (0, 2)]
+        chosen = jnp.stack([held["tables"][r] for r in order + [r | 1 for r in order]])
+        return chosen[:, :, 0].reshape(-1, rows), chosen[:, :, 1].reshape(-1, rows)
+
+    def hidden_of(groups, *earlier):
+        own = [held[group | q] for group in groups for q in range(4)]
+        others = [held["c", group] for group in groups]
+        return run_hidden(own, others, after(tables_of(groups)[0], *earlier), w_gate, w_up, slots)
+
+    def outputs_of(groups, hidden, *earlier):
+        pos, weight = tables_of(groups)
+        mine, *others = run_outputs(hidden, after(pos, *earlier), weight, w_down, slots, half)
+        return mine.reshape(-1, 4, rows, half), others
+
+    sums, received = {}, {}
+
+    def add_swapped(groups, mine, others, *earlier):
+        for n, group in enumerate(groups):
+            back = received["c", group] = hop(after(others[n], *earlier), "core")
+            back = back.reshape(4, rows, half)
+            for q in range(4):
+                at = jnp.where(core == 0, q, (q % 2) * 2 + q // 2)
+                sums[group | q] = [lax.dynamic_index_in_dim(v, at, 0, keepdims=False) for v in (mine[n], back)]
+
+    def total(j):
+        terms = sums[j] + [received[k] for k in SPREAD if k & ~BIT[HOP[k]] == j]
+        return sum(t.astype(F32) for t in terms).astype(BF16)
+
+    def spread_all(plan, *fence):
+        for j, earlier in plan:
+            earlier = [held[k] for k in earlier] + list(fence)
+            if j == "tables":
+                held[j] = tables_after(*earlier)
+            elif isinstance(j, tuple):
+                pieces = [after(held[j[1] | q], *earlier) if q else held[j[1]] for q in range(4)]
+                held[j] = hop(jnp.stack(pieces), "core")
+            else:
+                held[j] = hop(after(held[j & ~BIT[HOP[j]]], *earlier), HOP[j])
+
+    def collect_all(plan, *fence):
+        for j, earlier in plan:
+            earlier = [received[k] for k in earlier] + list(fence)
+            received[j] = hop(after(total(j), *earlier), HOP[j])
+
+    spread_all(SPREAD_AFTER)
+    near = hidden_of((0, 4))
+    spread_all([(("c", 8), ()), (("c", 12), ())], near)
+    far = hidden_of((12, 8))
+    mine, others = outputs_of((12, 8), far)
+    add_swapped((12, 8), mine, others)
+    mine, others = outputs_of((0, 4), near, received["c", 12])
+    add_swapped((0, 4), mine, others)
+    collect_all(COLLECT_AFTER)
+    return total(0)
 
 
 def on_device(tokens, expert_ids, gate_prob, w_gate, w_up, w_down):
@@ -61,6 +433,5 @@
         P("dp", "expert", None),
     )
     out_specs = P("dp", "expert")
-    return jax.shard_map(
-        on_device, mesh=mesh, in_specs=in_specs, out_specs=out_specs, check_vma=False
-    )
+    plan = on_block if (mesh.shape["dp"], mesh.shape["expert"]) == (16, 2) else on_device
+    return jax.shard_map(plan, mesh=mesh, in_specs=in_specs, out_specs=out_specs, check_vma=False)

time: 718 us -> 212 us (0.30)
  blocking collectives: 278 us -> 0 us
  waiting for transfers between devices: 302 us -> 82.3 us
  Pallas kernels: 0 us -> 57.6 us
  matrix products: 51.1 us -> 0.2 us
  local copies, waits for them, and re-layouts: 43.5 us -> 7.47 us
  starting transfers between devices: 6.55 us -> 40.7 us
  between operations: 13.5 us -> 0.33 us
    all_to_all x1 -> x0, blocking collectives: 278 us -> none  [on_device(): lax.all_to_all(padded[source_row].reshape(dp_count, local_experts, capaci...]
    all_to_all x1, waiting for transfers between devices: 223 us -> 0.01 us  [tables_after(): lax.all_to_all(own.reshape(dp_count, experts, 2, rows), 'dp', split_axis=...]
    ppermute x0 -> x38, waiting for transfers between devices: none -> 82.3 us  [hop(): return lax.ppermute(value, AXES, link_pairs(link))]
    reduce_scatter x1 -> x0, waiting for transfers between devices: 68.2 us -> none  [on_device(): lax.psum_scatter(jnp.sum(scaled.reshape(tok_rows, TOP, returned.shape[3])...]
    pallas_call x0 -> x4, Pallas kernels: none -> 57.6 us  [the longest x2 33.8 us: run_hidden(): pl.pallas_call(functools.partial(hidden_kernel, slots, ring), out_shape=j...]
    dot_general x3 -> x1, matrix products: 51.1 us -> 0.2 us  [slot_tables(): before = jnp.dot(earlier, chosen.astype(BF16), preferred_element_type=F32)]
    ppermute x0 -> x38, starting transfers between devices: none -> 37 us  [hop(): return lax.ppermute(value, AXES, link_pairs(link))]
    gather x2 -> x1, local copies, waits for them, and re-layouts: 30.9 us -> 0.59 us  [tables_after(): return every[me ^ jnp.arange(dp_count, dtype=jnp.int32)]]
  transfers between devices with their start and end apart: 3 -> 39, of which waited for: 3 -> 20; matrix products, arithmetic and copies ran while one was open for 2% -> 12% of each run, Pallas kernels for 0% -> 14%
where the time goes in v2:
time: 212 us; the launch traced here: 211 us
  waiting for transfers between devices  82.3 us (39%)
  Pallas kernels  57.6 us (27%)
  starting transfers between devices  40.7 us (19%)
  other arithmetic  22.8 us (11%)
  local copies, waits for them, and re-layouts  7.47 us (4%)
    ppermute x38, waiting for transfers between devices, hop(): return lax.ppermute(value, AXES, link_pairs(link))  82.3 us
    ppermute x38, starting transfers between devices, hop(): return lax.ppermute(value, AXES, link_pairs(link))  37 us
    pallas_call x2, Pallas kernels, run_hidden(): pl.pallas_call(functools.partial(hidden_kernel, slots, ring), out_shape=j...  33.8 us
    pallas_call x2, Pallas kernels, run_outputs(): pl.pallas_call(functools.partial(output_kernel, slots, groups), out_shape...  23.8 us
    convert_element_type x12, other arithmetic, total(): return sum((t.astype(F32) for t in terms)).astype(BF16)  12.6 us
    another operation x4, other arithmetic, spread_all(): held[j] = hop(jnp.stack(pieces), 'core')  8.72 us
  transfers between devices with their start and end apart: 39, of which 20 were waited for; matrix products, arithmetic and copies ran while one was open for 12% of the time, Pallas kernels for 14%

profile of v2, /device:TPU:0, one launch (start us, length us, event | category | flops | bytes accessed | tf_op | source)
XLA Modules:
  0.0 211.4 jit_solution(4718384039854530838)
XLA Ops:
  0.0 2.9 %collective-permute-start.1 = (bf16[128,2048]{1,0:T(8,128)(2,1)}, bf16[128,2048]{1,0:T(8,128)(2,1)S(1)}, u32[]{:S(2)}, u32[]{:S(2)}) collective-permute-start(bf16[128,2048]{1,0:T(8,128)(2,1)} %refs_0_.1), channel_id=1, source_target_pairs={{0,4},{1,5},{2,3},{3,2},{4,0},{5,1},{6,7},{7,6},{8,12},{9,13},{10,... | collective-permute-start | bytes 1572872 | tf_op jit(solution)/shard_map/ppermute | solution.py:30
  7.1 3.2 %collective-permute-done.1.refs_2_ = bf16[128,2048]{1,0:T(8,128)(2,1)S(1)} collective-permute-done((bf16[128,2048]{1,0:T(8,128)(2,1)}, bf16[128,2048]{1,0:T(8,128)(2,1)S(1)}, u32[]{:S(2)}, u32[]{:S(2)}) %collective-permute-start.1) | collective-permute-done | bytes 524320 | tf_op jit(solution)/shard_map/ppermute | solution.py:30
  13.3 15.5 %collective-permute-done.2.refs_4_ = bf16[128,2048]{1,0:T(8,128)(2,1)S(1)} collective-permute-done((bf16[128,2048]{1,0:T(8,128)(2,1)}, bf16[128,2048]{1,0:T(8,128)(2,1)S(1)}, u32[]{:S(2)}, u32[]{:S(2)}) %collective-permute-start.2) | collective-permute-done | bytes 524320 | tf_op jit(solution)/shard_map/ppermute | solution.py:30
  33.8 3.7 %all-to-all-start = ((f32[16,2,2,128]{3,2,1,0:T(2,128)}), f32[16,2,2,128]{3,2,1,0:T(2,128)S(1)}, u32[]{:S(2)}, u32[]{:S(2)}) async-start(f32[16,2,2,128]{3,2,1,0:T(2,128)} %copy.12), calls=%async_computation | async-start | bytes 65536 | tf_op jit(solution)/shard_map/all_to_all | solution.py:319
  37.5 2.7 %pad_maximum_fusion = bf16[4,128,2048]{2,1,0:T(8,128)(2,1)} fusion(bf16[1,128,2048]{2,1,0:T(8,128)(2,1)S(1)} %bitcast.105, bf16[1,128,2048]{2,1,0:T(8,128)(2,1)S(1)} %bitcast.103, bf16[1,128,2048]{2,1,0:T(8,128)(2,1)S(1)} %bitcast.106, bf16[1,128,2048]{2,1,0:T(8,128)(2,1)} %bitcast.101), kind=kLoop, calls=%fused_computation.1 | loop fusion | flops 3145728 | bytes 4194304 | tf_op jit(solution)/shard_map/stack | solution.py:360
  40.6 3.2 %collective-permute-done.6.refs_5_ = bf16[128,2048]{1,0:T(8,128)(2,1)S(1)} collective-permute-done((bf16[128,2048]{1,0:T(8,128)(2,1)S(1)}, bf16[128,2048]{1,0:T(8,128)(2,1)S(1)}, u32[]{:S(2)}, u32[]{:S(2)}) %collective-permute-start.6) | collective-permute-done | bytes 524320 | tf_op jit(solution)/shard_map/ppermute | solution.py:30
  44.6 3.0 %pad_maximum_fusion.1 = bf16[4,128,2048]{2,1,0:T(8,128)(2,1)} fusion(bf16[1,128,2048]{2,1,0:T(8,128)(2,1)} %bitcast.17, bf16[1,128,2048]{2,1,0:T(8,128)(2,1)} %bitcast.16, bf16[1,128,2048]{2,1,0:T(8,128)(2,1)} %bitcast.107, bf16[1,128,2048]{2,1,0:T(8,128)(2,1)S(1)} %bitcast.104), kind=kLoop, calls=%fused_computation.2 | loop fusion | flops 3145728 | bytes 4194304 | tf_op jit(solution)/shard_map/stack | solution.py:360
  50.1 6.9 %collective-permute-done.5.refs_6_ = bf16[128,2048]{1,0:T(8,128)(2,1)} collective-permute-done((bf16[128,2048]{1,0:T(8,128)(2,1)S(1)}, bf16[128,2048]{1,0:T(8,128)(2,1)}, u32[]{:S(2)}, u32[]{:S(2)}) %collective-permute-start.5) | collective-permute-done | bytes 524320 | tf_op jit(solution)/shard_map/ppermute | solution.py:30
  59.1 3.6 %collective-permute-done.3.refs_0_ = bf16[128,2048]{1,0:T(8,128)(2,1)} collective-permute-done((bf16[128,2048]{1,0:T(8,128)(2,1)S(1)}, bf16[128,2048]{1,0:T(8,128)(2,1)}, u32[]{:S(2)}, u32[]{:S(2)}) %collective-permute-start.3) | collective-permute-done | bytes 524320 | tf_op jit(solution)/shard_map/ppermute | solution.py:30
  62.7 3.7 %collective-permute-done.7.refs_7_ = bf16[128,2048]{1,0:T(8,128)(2,1)S(1)} collective-permute-done((bf16[128,2048]{1,0:T(8,128)(2,1)}, bf16[128,2048]{1,0:T(8,128)(2,1)S(1)}, u32[]{:S(2)}, u32[]{:S(2)}) %collective-permute-start.7) | collective-permute-done | bytes 524320 | tf_op jit(solution)/shard_map/ppermute | solution.py:30
  70.5 17.0 %hidden_units.2.refs_2_ = bf16[2,384,768]{2,1,0:T(8,128)(2,1)S(1)} custom-call(bf16[128,2048]{1,0:T(8,128)(2,1)S(1)} %copy-done, bf16[128,2048]{1,0:T(8,128)(2,1)S(1)} %collective-permute-done.refs_1_, bf16[128,2048]{1,0:T(8,128)(2,1)S(1)} %collective-permute-done.1.refs_2_, bf16[128,2048]{1,0:T(8,128)(2,1)S(1)} %collective-permute-done.11.refs_3_, ...), custom_call_target="tpu_custom_call" | custom-call | flops 9663676416 | bytes 33554432 | tf_op jit(solution)/shard_map/hidden_units/pallas_call | solution.py:190
  93.5 3.0 %collective-permute-done.17.refs_8_ = bf16[4,128,2048]{2,1,0:T(8,128)(2,1)S(1)} collective-permute-done((bf16[4,128,2048]{2,1,0:T(8,128)(2,1)S(1)}, bf16[4,128,2048]{2,1,0:T(8,128)(2,1)S(1)}, u32[]{:S(2)}, u32[]{:S(2)}) %collective-permute-start.17) | collective-permute-done | bytes 2097184 | tf_op jit(solution)/shard_map/ppermute | solution.py:30
  97.8 16.8 %hidden_units.3.refs_2_ = bf16[2,384,768]{2,1,0:T(8,128)(2,1)S(1)} custom-call(bf16[128,2048]{1,0:T(8,128)(2,1)} %collective-permute-done.3.refs_0_, bf16[128,2048]{1,0:T(8,128)(2,1)S(1)} %collective-permute-done.9.refs_1_, bf16[128,2048]{1,0:T(8,128)(2,1)S(1)} %collective-permute-done.10.refs_2_, bf16[128,2048]{1,0:T(8,128)(2,1)S(1)} %collective-permute-done.13.refs_3_, ...), custom_call_target="tpu_custom_call" | custom-call | flops 9663676416 | bytes 33554432 | tf_op jit(solution)/shard_map/hidden_units/pallas_call | solution.py:190
  114.6 11.9 %weighted_outputs.2 = (bf16[4,2,128,2048]{3,2,1,0:T(8,128)(2,1)}, bf16[2,2,128,2048]{3,2,1,0:T(8,128)(2,1)}, bf16[2,2,128,2048]{3,2,1,0:T(8,128)(2,1)S(1)}) custom-call(f32[16,128]{1,0:T(8,128)S(1)} %bitcast.117, f32[16,128]{1,0:T(8,128)S(1)} %bitcast.118, bf16[2,384,768]{2,1,0:T(8,128)(2,1)S(1)} %hidden_units.3.refs_2_, bf16[2,768,4096]{2,1,0:T(8,128)(2,1)} %refs_3_.3), custom_call_target="tpu_custom_call" | custom-call | flops 4831838208 | bytes 20971520 | tf_op jit(solution)/shard_map/weighted_outputs/pallas_call | solution.py:226
  127.1 2.8 %fusion.33 = (bf16[2,2,128,2048]{3,2,1,0:T(8,128)(2,1)S(1)}, bf16[2,2,128,2048]{3,2,1,0:T(8,128)(2,1)S(1)}) fusion(bf16[4,2,128,2048]{3,2,1,0:T(8,128)(2,1)} %get-tuple-element.44), kind=kLoop, calls=%fused_computation.77 | loop fusion | bytes 8388608 | tf_op jit(solution)/shard_map/slice | solution.py:347
  129.9 2.9 %collective-permute-done.19 = bf16[2,2,128,2048]{3,2,1,0:T(8,128)(2,1)} collective-permute-done((bf16[2,2,128,2048]{3,2,1,0:T(8,128)(2,1)}, bf16[2,2,128,2048]{3,2,1,0:T(8,128)(2,1)}, u32[]{:S(2)}, u32[]{:S(2)}) %collective-permute-start.19) | collective-permute-done | bytes 2097184 | tf_op jit(solution)/shard_map/ppermute | solution.py:30
  132.8 2.9 %fusion.17 = (bf16[128,2048]{1,0:T(8,128)(2,1)}, bf16[128,2048]{1,0:T(8,128)(2,1)S(1)}, bf16[128,2048]{1,0:T(8,128)(2,1)S(1)}) fusion(bf16[4,128,2048]{2,1,0:T(8,128)(2,1)} %bitcast.36, bf16[4,128,2048]{2,1,0:T(8,128)(2,1)S(1)} %bitcast.125, s32[]{:T(128)S(6)} %select_n.90, s32[]{:T(128)S(6)} %select_n.89), kind=kLoop, calls=%fused_computation.39 | loop fusion | flops 3145728 | bytes 4718600 | tf_op jit(solution)/shard_map/convert_element_type | solution.py:351
  138.7 11.9 %weighted_outputs.3 = (bf16[4,2,128,2048]{3,2,1,0:T(8,128)(2,1)}, bf16[2,2,128,2048]{3,2,1,0:T(8,128)(2,1)S(1)}, bf16[2,2,128,2048]{3,2,1,0:T(8,128)(2,1)S(1)}) custom-call(f32[16,128]{1,0:T(8,128)S(1)} %bitcast.115, f32[16,128]{1,0:T(8,128)S(1)} %bitcast.113, bf16[2,384,768]{2,1,0:T(8,128)(2,1)S(1)} %copy-done.4, bf16[2,768,4096]{2,1,0:T(8,128)(2,1)} %refs_3_.3), custom_call_target="tpu_custom_call" | custom-call | flops 4831838208 | bytes 20971520 | tf_op jit(solution)/shard_map/weighted_outputs/pallas_call | solution.py:226
  158.5 2.9 %collective-permute-done.24 = bf16[128,2048]{1,0:T(8,128)(2,1)S(1)} collective-permute-done((bf16[128,2048]{1,0:T(8,128)(2,1)S(1)}, bf16[128,2048]{1,0:T(8,128)(2,1)S(1)}, u32[]{:S(2)}, u32[]{:S(2)}) %collective-permute-start.24) | collective-permute-done | bytes 524320 | tf_op jit(solution)/shard_map/ppermute | solution.py:30
  165.8 3.2 %collective-permute-done.22 = bf16[128,2048]{1,0:T(8,128)(2,1)S(1)} collective-permute-done((bf16[128,2048]{1,0:T(8,128)(2,1)S(1)}, bf16[128,2048]{1,0:T(8,128)(2,1)S(1)}, u32[]{:S(2)}, u32[]{:S(2)}) %collective-permute-start.22) | collective-permute-done | bytes 524320 | tf_op jit(solution)/shard_map/ppermute | solution.py:30
  169.0 2.9 %collective-permute-done.28 = bf16[128,2048]{1,0:T(8,128)(2,1)S(1)} collective-permute-done((bf16[128,2048]{1,0:T(8,128)(2,1)S(1)}, bf16[128,2048]{1,0:T(8,128)(2,1)S(1)}, u32[]{:S(2)}, u32[]{:S(2)}) %collective-permute-start.28) | collective-permute-done | bytes 524320 | tf_op jit(solution)/shard_map/ppermute | solution.py:30
  177.8 11.9 %collective-permute-done.35 = bf16[128,2048]{1,0:T(8,128)(2,1)S(1)} collective-permute-done((bf16[128,2048]{1,0:T(8,128)(2,1)S(1)}, bf16[128,2048]{1,0:T(8,128)(2,1)S(1)}, u32[]{:S(2)}, u32[]{:S(2)}) %collective-permute-start.35) | collective-permute-done | bytes 524320 | tf_op jit(solution)/shard_map/ppermute | solution.py:30
  192.6 6.5 %collective-permute-done.36 = bf16[128,2048]{1,0:T(8,128)(2,1)S(1)} collective-permute-done((bf16[128,2048]{1,0:T(8,128)(2,1)S(1)}, bf16[128,2048]{1,0:T(8,128)(2,1)S(1)}, u32[]{:S(2)}, u32[]{:S(2)}) %collective-permute-start.36) | collective-permute-done | bytes 524320 | tf_op jit(solution)/shard_map/ppermute | solution.py:30
  200.4 8.1 %collective-permute-done.34 = bf16[128,2048]{1,0:T(8,128)(2,1)S(1)} collective-permute-done((bf16[128,2048]{1,0:T(8,128)(2,1)S(1)}, bf16[128,2048]{1,0:T(8,128)(2,1)S(1)}, u32[]{:S(2)}, u32[]{:S(2)}) %collective-permute-start.34) | collective-permute-done | bytes 524320 | tf_op jit(solution)/shard_map/ppermute | solution.py:30
  (110 shorter events, 58.1 us)
Async XLA Ops:
  2.9 25.9 %collective-permute-start.2 = (bf16[128,2048]{1,0:T(8,128)(2,1)}, bf16[128,2048]{1,0:T(8,128)(2,1)S(1)}, u32[]{:S(2)}, u32[]{:S(2)}) collective-permute-start(bf16[128,2048]{1,0:T(8,128)(2,1)} %refs_0_.1), channel_id=1, source_target_pairs={{0,16},{1,17},{2,18},{3,19},{4,20},{5,21},{6,22},{7,23},{8,24},{9,... | collective-permute-start | bytes 1572872 | tf_op jit(solution)/shard_map/ppermute | solution.py:30
  5.5 23.5 %collective-permute-start.4 = (bf16[128,2048]{1,0:T(8,128)(2,1)}, bf16[128,2048]{1,0:T(8,128)(2,1)S(1)}, u32[]{:S(2)}, u32[]{:S(2)}) collective-permute-start(bf16[128,2048]{1,0:T(8,128)(2,1)} %refs_0_.1), channel_id=1, source_target_pairs={{0,8},{1,9},{2,10},{3,11},{4,12},{5,13},{6,14},{7,15},{8,0},{9,1},... | collective-permute-start | bytes 1572872 | tf_op jit(solution)/shard_map/ppermute | solution.py:30
  10.3 20.7 %collective-permute-start.11 = (bf16[128,2048]{1,0:T(8,128)(2,1)S(1)}, bf16[128,2048]{1,0:T(8,128)(2,1)S(1)}, u32[]{:S(2)}, u32[]{:S(2)}) collective-permute-start(bf16[128,2048]{1,0:T(8,128)(2,1)S(1)} %collective-permute-done.1.refs_2_), channel_id=1, source_target_pairs={{0,1},{1,0},{2,6},{3,7},{4,5},{5,4},{6,2},{7,3},{8,9},{9,8},{10,14... | collective-permute-start | bytes 1572872 | tf_op jit(solution)/shard_map/ppermute | solution.py:30
  12.4 20.8 %collective-permute-start = (bf16[128,2048]{1,0:T(8,128)(2,1)}, bf16[128,2048]{1,0:T(8,128)(2,1)S(1)}, u32[]{:S(2)}, u32[]{:S(2)}) collective-permute-start(bf16[128,2048]{1,0:T(8,128)(2,1)} %refs_0_.1), channel_id=1, source_target_pairs={{0,1},{1,0},{2,6},{3,7},{4,5},{5,4},{6,2},{7,3},{8,9},{9,8},{10,14... | collective-permute-start | bytes 1572872 | tf_op jit(solution)/shard_map/ppermute | solution.py:30
  29.0 14.8 %collective-permute-start.6 = (bf16[128,2048]{1,0:T(8,128)(2,1)S(1)}, bf16[128,2048]{1,0:T(8,128)(2,1)S(1)}, u32[]{:S(2)}, u32[]{:S(2)}) collective-permute-start(bf16[128,2048]{1,0:T(8,128)(2,1)S(1)} %collective-permute-done.4.refs_4_), channel_id=1, source_target_pairs={{0,1},{1,0},{2,6},{3,7},{4,5},{5,4},{6,2},{7,3},{8,9},{9,8},{10,14... | collective-permute-start | bytes 1572872 | tf_op jit(solution)/shard_map/ppermute | solution.py:30
  33.8 15.6 %all-to-all-start = ((f32[16,2,2,128]{3,2,1,0:T(2,128)}), f32[16,2,2,128]{3,2,1,0:T(2,128)S(1)}, u32[]{:S(2)}, u32[]{:S(2)}) async-start(f32[16,2,2,128]{3,2,1,0:T(2,128)} %copy.12), calls=%async_computation | async-start | bytes 65536 | tf_op jit(solution)/shard_map/all_to_all | solution.py:319
  40.2 27.8 %collective-permute-start.15 = (bf16[4,128,2048]{2,1,0:T(8,128)(2,1)}, bf16[4,128,2048]{2,1,0:T(8,128)(2,1)}, u32[]{:S(2)}, u32[]{:S(2)}) collective-permute-start(bf16[4,128,2048]{2,1,0:T(8,128)(2,1)} %pad_maximum_fusion), channel_id=1, source_target_pairs={{0,2},{1,3},{2,0},{3,1},{4,6},{5,7},{6,4},{7,5},{8,10},{9,11},{10,... | collective-permute-start | bytes 6291464 | tf_op jit(solution)/shard_map/ppermute | solution.py:30
  47.6 21.8 %collective-permute-start.16 = (bf16[4,128,2048]{2,1,0:T(8,128)(2,1)}, bf16[4,128,2048]{2,1,0:T(8,128)(2,1)}, u32[]{:S(2)}, u32[]{:S(2)}) collective-permute-start(bf16[4,128,2048]{2,1,0:T(8,128)(2,1)} %pad_maximum_fusion.1), channel_id=1, source_target_pairs={{0,2},{1,3},{2,0},{3,1},{4,6},{5,7},{6,4},{7,5},{8,10},{9,11},{10,... | collective-permute-start | bytes 6291464 | tf_op jit(solution)/shard_map/ppermute | solution.py:30
  58.4 29.1 %collective-permute-start.14 = (bf16[128,2048]{1,0:T(8,128)(2,1)S(1)}, bf16[128,2048]{1,0:T(8,128)(2,1)S(1)}, u32[]{:S(2)}, u32[]{:S(2)}) collective-permute-start(bf16[128,2048]{1,0:T(8,128)(2,1)S(1)} %collective-permute-done.2.refs_4_), channel_id=1, source_target_pairs={{0,1},{1,0},{2,6},{3,7},{4,5},{5,4},{6,2},{7,3},{8,9},{9,8},{10,14... | collective-permute-start | bytes 1572872 | tf_op jit(solution)/shard_map/ppermute | solution.py:30
  66.4 22.9 %collective-permute-start.9 = (bf16[128,2048]{1,0:T(8,128)(2,1)}, bf16[128,2048]{1,0:T(8,128)(2,1)S(1)}, u32[]{:S(2)}, u32[]{:S(2)}) collective-permute-start(bf16[128,2048]{1,0:T(8,128)(2,1)} %collective-permute-done.3.refs_0_), channel_id=1, source_target_pairs={{0,1},{1,0},{2,6},{3,7},{4,5},{5,4},{6,2},{7,3},{8,9},{9,8},{10,14... | collective-permute-start | bytes 1572872 | tf_op jit(solution)/shard_map/ppermute | solution.py:30
  67.7 21.6 %collective-permute-start.10 = (bf16[128,2048]{1,0:T(8,128)(2,1)}, bf16[128,2048]{1,0:T(8,128)(2,1)S(1)}, u32[]{:S(2)}, u32[]{:S(2)}) collective-permute-start(bf16[128,2048]{1,0:T(8,128)(2,1)} %collective-permute-done.3.refs_0_), channel_id=1, source_target_pairs={{0,4},{1,5},{2,3},{3,2},{4,0},{5,1},{6,7},{7,6},{8,12},{9,13},{10,... | collective-permute-start | bytes 1572872 | tf_op jit(solution)/shard_map/ppermute | solution.py:30
  68.0 21.3 %collective-permute-start.13 = (bf16[128,2048]{1,0:T(8,128)(2,1)S(1)}, bf16[128,2048]{1,0:T(8,128)(2,1)S(1)}, u32[]{:S(2)}, u32[]{:S(2)}) collective-permute-start(bf16[128,2048]{1,0:T(8,128)(2,1)S(1)} %collective-permute-done.7.refs_7_), channel_id=1, source_target_pairs={{0,8},{1,9},{2,10},{3,11},{4,12},{5,13},{6,14},{7,15},{8,0},{9,1},... | collective-permute-start | bytes 1572872 | tf_op jit(solution)/shard_map/ppermute | solution.py:30
  126.7 24.0 %collective-permute-start.21 = (bf16[2,2,128,2048]{3,2,1,0:T(8,128)(2,1)S(1)}, bf16[2,2,128,2048]{3,2,1,0:T(8,128)(2,1)}, u32[]{:S(2)}, u32[]{:S(2)}) collective-permute-start(bf16[2,2,128,2048]{3,2,1,0:T(8,128)(2,1)S(1)} %get-tuple-element.45), channel_id=1, source_target_pairs={{0,2},{1,3},{2,0},{3,1},{4,6},{5,7},{6,4},{7,5},{8,10},{9,11},{10,... | collective-permute-start | bytes 6291464 | tf_op jit(solution)/shard_map/ppermute | solution.py:30
  135.7 15.0 %collective-permute-start.23 = (bf16[128,2048]{1,0:T(8,128)(2,1)}, bf16[128,2048]{1,0:T(8,128)(2,1)}, u32[]{:S(2)}, u32[]{:S(2)}) collective-permute-start(bf16[128,2048]{1,0:T(8,128)(2,1)} %get-tuple-element.49), channel_id=1, source_target_pairs={{0,8},{1,9},{2,10},{3,11},{4,12},{5,13},{6,14},{7,15},{8,0},{9,1},... | collective-permute-start | bytes 1572872 | tf_op jit(solution)/shard_map/ppermute | solution.py:30
  136.1 19.3 %collective-permute-start.26 = (bf16[128,2048]{1,0:T(8,128)(2,1)S(1)}, bf16[128,2048]{1,0:T(8,128)(2,1)S(1)}, u32[]{:S(2)}, u32[]{:S(2)}) collective-permute-start(bf16[128,2048]{1,0:T(8,128)(2,1)S(1)} %get-tuple-element.51), channel_id=1, source_target_pairs={{0,1},{1,0},{2,6},{3,7},{4,5},{5,4},{6,2},{7,3},{8,9},{9,8},{10,14... | collective-permute-start | bytes 1572872 | tf_op jit(solution)/shard_map/ppermute | solution.py:30
  136.9 18.6 %collective-permute-start.27 = (bf16[128,2048]{1,0:T(8,128)(2,1)S(1)}, bf16[128,2048]{1,0:T(8,128)(2,1)S(1)}, u32[]{:S(2)}, u32[]{:S(2)}) collective-permute-start(bf16[128,2048]{1,0:T(8,128)(2,1)S(1)} %get-tuple-element.50), channel_id=1, source_target_pairs={{0,4},{1,5},{2,3},{3,2},{4,0},{5,1},{6,7},{7,6},{8,12},{9,13},{10,... | collective-permute-start | bytes 1572872 | tf_op jit(solution)/shard_map/ppermute | solution.py:30
  155.5 22.3 %collective-permute-start.20 = (bf16[2,2,128,2048]{3,2,1,0:T(8,128)(2,1)S(1)}, bf16[2,2,128,2048]{3,2,1,0:T(8,128)(2,1)S(1)}, u32[]{:S(2)}, u32[]{:S(2)}) collective-permute-start(bf16[2,2,128,2048]{3,2,1,0:T(8,128)(2,1)S(1)} %get-tuple-element.43), channel_id=1, source_target_pairs={{0,2},{1,3},{2,0},{3,1},{4,6},{5,7},{6,4},{7,5},{8,10},{9,11},{10,... | collective-permute-start | bytes 6291464 | tf_op jit(solution)/shard_map/ppermute | solution.py:30
  157.0 14.9 %collective-permute-start.28 = (bf16[128,2048]{1,0:T(8,128)(2,1)S(1)}, bf16[128,2048]{1,0:T(8,128)(2,1)S(1)}, u32[]{:S(2)}, u32[]{:S(2)}) collective-permute-start(bf16[128,2048]{1,0:T(8,128)(2,1)S(1)} %fusion.6), channel_id=1, source_target_pairs={{0,8},{1,9},{2,10},{3,11},{4,12},{5,13},{6,14},{7,15},{8,0},{9,1},... | collective-permute-start | bytes 1572872 | tf_op jit(solution)/shard_map/ppermute | solution.py:30
  164.9 24.7 %collective-permute-start.35 = (bf16[128,2048]{1,0:T(8,128)(2,1)S(1)}, bf16[128,2048]{1,0:T(8,128)(2,1)S(1)}, u32[]{:S(2)}, u32[]{:S(2)}) collective-permute-start(bf16[128,2048]{1,0:T(8,128)(2,1)S(1)} %get-tuple-element.53), channel_id=1, source_target_pairs={{0,8},{1,9},{2,10},{3,11},{4,12},{5,13},{6,14},{7,15},{8,0},{9,1},... | collective-permute-start | bytes 1572872 | tf_op jit(solution)/shard_map/ppermute | solution.py:30
  173.6 26.8 %collective-permute-start.29 = (bf16[128,2048]{1,0:T(8,128)(2,1)S(1)}, bf16[128,2048]{1,0:T(8,128)(2,1)S(1)}, u32[]{:S(2)}, u32[]{:S(2)}) collective-permute-start(bf16[128,2048]{1,0:T(8,128)(2,1)S(1)} %fusion.11), channel_id=1, source_target_pairs={{0,16},{1,17},{2,18},{3,19},{4,20},{5,21},{6,22},{7,23},{8,24},{9,... | collective-permute-start | bytes 1572872 | tf_op jit(solution)/shard_map/ppermute | solution.py:30
  175.7 16.4 %collective-permute-start.31 = (bf16[128,2048]{1,0:T(8,128)(2,1)S(1)}, bf16[128,2048]{1,0:T(8,128)(2,1)S(1)}, u32[]{:S(2)}, u32[]{:S(2)}) collective-permute-start(bf16[128,2048]{1,0:T(8,128)(2,1)S(1)} %get-tuple-element.52), channel_id=1, source_target_pairs={{0,1},{1,0},{2,6},{3,7},{4,5},{5,4},{6,2},{7,3},{8,9},{9,8},{10,14... | collective-permute-start | bytes 1572872 | tf_op jit(solution)/shard_map/ppermute | solution.py:30
  177.4 14.8 %collective-permute-start.32 = (bf16[128,2048]{1,0:T(8,128)(2,1)S(1)}, bf16[128,2048]{1,0:T(8,128)(2,1)S(1)}, u32[]{:S(2)}, u32[]{:S(2)}) collective-permute-start(bf16[128,2048]{1,0:T(8,128)(2,1)S(1)} %get-tuple-element.54), channel_id=1, source_target_pairs={{0,4},{1,5},{2,3},{3,2},{4,0},{5,1},{6,7},{7,6},{8,12},{9,13},{10,... | collective-permute-start | bytes 1572872 | tf_op jit(solution)/shard_map/ppermute | solution.py:30
  191.5 17.0 %collective-permute-start.34 = (bf16[128,2048]{1,0:T(8,128)(2,1)S(1)}, bf16[128,2048]{1,0:T(8,128)(2,1)S(1)}, u32[]{:S(2)}, u32[]{:S(2)}) collective-permute-start(bf16[128,2048]{1,0:T(8,128)(2,1)S(1)} %fusion.22), channel_id=1, source_target_pairs={{0,1},{1,0},{2,6},{3,7},{4,5},{5,4},{6,2},{7,3},{8,9},{9,8},{10,14... | collective-permute-start | bytes 1572872 | tf_op jit(solution)/shard_map/ppermute | solution.py:30
  192.5 17.5 %collective-permute-start.33 = (bf16[128,2048]{1,0:T(8,128)(2,1)S(1)}, bf16[128,2048]{1,0:T(8,128)(2,1)S(1)}, u32[]{:S(2)}, u32[]{:S(2)}) collective-permute-start(bf16[128,2048]{1,0:T(8,128)(2,1)S(1)} %fusion.4), channel_id=1, source_target_pairs={{0,8},{1,9},{2,10},{3,11},{4,12},{5,13},{6,14},{7,15},{8,0},{9,1},... | collective-permute-start | bytes 1572872 | tf_op jit(solution)/shard_map/ppermute | solution.py:30
  (23 other events, 201.0 us)

commit v3 on v2

--- a/solution.py
+++ b/solution.py
@@ -35,17 +35,17 @@
 
 
 def hidden_kernel(slots, ring, *refs):
-    groups = (len(refs) - 14) // 5
+    groups = (len(refs) - 13) // 5
     count = 8 * groups
     own, across, refs = refs[: 4 * groups], refs[4 * groups : 5 * groups], refs[5 * groups :]
     pieces = list(own) + [a.at[q] for a in across for q in range(4)]
     (pos, w_gate, w_up, out), scratch = refs[:4], refs[4:]
-    held, gates, ups, routed, hidden, pick, piece_sem, gate_sem, up_sem, out_sem = scratch
+    held, both, routed, hidden, pick, piece_sem, gate_sem, up_sem, out_sem = scratch
     core, side = lax.axis_index("dp") % 2, lax.axis_index("expert")
     experts, hid, width = w_gate.shape
     rows, half = pieces[0].shape
     blocks = count // 2
-    hid_block = gates.shape[1]
+    hid_block = both.shape[1] // 2
     per_expert = hid // hid_block
     hid_steps = experts * per_expert
 
@@ -55,8 +55,8 @@
     def weight_copies(i):
         at, slot = pl.ds((i % per_expert) * hid_block, hid_block), i % ring
         return (
-            pltpu.make_async_copy(w_gate.at[i // per_expert, at], gates.at[slot], gate_sem.at[slot]),
-            pltpu.make_async_copy(w_up.at[i // per_expert, at], ups.at[slot], up_sem.at[slot]),
+            pltpu.make_async_copy(w_gate.at[i // per_expert, at], both.at[slot, pl.ds(0, hid_block)], gate_sem.at[slot]),
+            pltpu.make_async_copy(w_up.at[i // per_expert, at], both.at[slot, pl.ds(hid_block, hid_block)], up_sem.at[slot]),
         )
 
     for i in range(count):
@@ -93,8 +93,8 @@
         e, slot = i // per_expert, i % ring
         at = pl.multiple_of((i % per_expert) * hid_block, hid_block)
         contract = (((1,), (1,)), ((), ()))
-        gate = lax.dot_general(routed[e], gates[slot], contract, preferred_element_type=F32)
-        up = lax.dot_general(routed[e], ups[slot], contract, preferred_element_type=F32)
+        gate_up = lax.dot_general(routed[e], both[slot], contract, preferred_element_type=F32)
+        gate, up = gate_up[:, :hid_block], gate_up[:, hid_block:]
         hidden[e, :, pl.ds(at, hid_block)] = (silu(gate) * up).astype(BF16)
 
         @pl.when(i + ring < hid_steps)
@@ -194,8 +194,7 @@
         out_specs=ANYWHERE,
         scratch_shapes=[
             pltpu.VMEM((count, rows, half), BF16),
-            pltpu.VMEM((ring, hid_block, width), BF16),
-            pltpu.VMEM((ring, hid_block, width), BF16),
+            pltpu.VMEM((ring, 2 * hid_block, width), BF16),
             pltpu.VMEM((experts, used, width), BF16),
             pltpu.VMEM((experts, used, hid), BF16),
             pltpu.VMEM((blocks, experts * slots, rows), BF16),
@@ -204,7 +203,7 @@
             pltpu.SemaphoreType.DMA((ring,)),
             pltpu.SemaphoreType.DMA,
         ],
-        compiler_params=pltpu.CompilerParams(vmem_limit_bytes=48 << 20),
+        compiler_params=pltpu.CompilerParams(vmem_limit_bytes=40 << 20),
         cost_estimate=pl.CostEstimate(
             flops=4 * experts * used * hid * width,
             bytes_accessed=4 * experts * hid * width + 2 * count * rows * half,
@@ -238,9 +237,9 @@
             pltpu.SemaphoreType.DMA((width // col_block,)),
             pltpu.SemaphoreType.DMA((2, 1 + groups)),
         ],
-        compiler_params=pltpu.CompilerParams(vmem_limit_bytes=48 << 20),
+        compiler_params=pltpu.CompilerParams(vmem_limit_bytes=40 << 20),
         cost_estimate=pl.CostEstimate(
-            flops=2 * experts * used * hid * width,
+            flops=16 * experts * used * hid * width,
             bytes_accessed=2 * experts * hid * width + 4 * blocks * rows * half,
             transcendentals=0,
         ),
@@ -266,12 +265,12 @@
     (1, ()),
     (3, ()),
     ('tables', (1, 2)),
-    (5, (8,)),
+    (5, (8, 'tables')),
     (6, (8,)),
     (10, (4,)),
     (12, ()),
     (7, (3, 8)),
-    (11, (5,)),
+    (11, ()),
     (('c', 0), ()),
     (9, (10, 5)),
     (('c', 4), ()),
@@ -286,10 +285,10 @@
     (14, ()),
     (9, ()),
     (11, ()),
-    (12, ()),
+    (12, (('c', 8),)),
     (7, ()),
     (5, ()),
-    (6, ()),
+    (6, (('c', 4), ('c', 8))),
     (10, ()),
     (8, ()),
     (1, ()),

time: 212 us -> 205 us (0.967)
  other arithmetic: 22.8 us -> 10.9 us
  starting transfers between devices: 40.7 us -> 46.7 us
    another operation x4, other arithmetic: 8.72 us -> 2.09 us  [spread_all(): held[j] = hop(jnp.stack(pieces), 'core')]
    convert_element_type x12, other arithmetic: 12.6 us -> 7.32 us  [total(): return sum((t.astype(F32) for t in terms)).astype(BF16)]
    all_to_all x1, starting transfers between devices: 3.7 us -> 7.88 us  [tables_after(): lax.all_to_all(own.reshape(dp_count, experts, 2, rows), 'dp', split_axis=...]
  transfers between devices with their start and end apart: 39 -> 39, of which waited for: 20 -> 21; matrix products, arithmetic and copies ran while one was open for 12% -> 7% of each run, Pallas kernels for 14% -> 14%
where the time goes in v3:
time: 205 us
  waiting for transfers between devices  83.2 us (41%)
  Pallas kernels  56.8 us (28%)
  starting transfers between devices  46.7 us (23%)
  other arithmetic  10.9 us (5%)
  local copies, waits for them, and re-layouts  6.81 us (3%)
    ppermute x38, waiting for transfers between devices, hop(): return lax.ppermute(value, AXES, link_pairs(link))  83.2 us
    ppermute x38, starting transfers between devices, hop(): return lax.ppermute(value, AXES, link_pairs(link))  38.8 us
    pallas_call x2, Pallas kernels, run_hidden(): pl.pallas_call(functools.partial(hidden_kernel, slots, ring), out_shape=j...  32.7 us
    pallas_call x2, Pallas kernels, run_outputs(): pl.pallas_call(functools.partial(output_kernel, slots, groups), out_shape...  24.1 us
    all_to_all x1, starting transfers between devices, tables_after(): lax.all_to_all(own.reshape(dp_count, experts, 2, rows), 'dp', split_axis=...  7.88 us
    convert_element_type x12, other arithmetic, total(): return sum((t.astype(F32) for t in terms)).astype(BF16)  7.32 us
  transfers between devices with their start and end apart: 39, of which 21 were waited for; matrix products, arithmetic and copies ran while one was open for 7% of the time, Pallas kernels for 14%

profile of v3, /device:TPU:0, one launch (start us, length us, event | category | flops | bytes accessed | tf_op | source)
XLA Modules:
  0.0 204.9 jit_solution(16942265197840913866)
XLA Ops:
  0.0 2.9 %collective-permute-start.1 = (bf16[128,2048]{1,0:T(8,128)(2,1)}, bf16[128,2048]{1,0:T(8,128)(2,1)S(1)}, u32[]{:S(2)}, u32[]{:S(2)}) collective-permute-start(bf16[128,2048]{1,0:T(8,128)(2,1)} %refs_0_.1), channel_id=1, source_target_pairs={{0,4},{1,5},{2,3},{3,2},{4,0},{5,1},{6,7},{7,6},{8,12},{9,13},{10,... | collective-permute-start | bytes 1572872 | tf_op jit(solution)/shard_map/ppermute | solution.py:30
  4.5 2.6 %collective-permute-start.2 = (bf16[128,2048]{1,0:T(8,128)(2,1)}, bf16[128,2048]{1,0:T(8,128)(2,1)S(1)}, u32[]{:S(2)}, u32[]{:S(2)}) collective-permute-start(bf16[128,2048]{1,0:T(8,128)(2,1)} %refs_0_.1), channel_id=1, source_target_pairs={{0,16},{1,17},{2,18},{3,19},{4,20},{5,21},{6,22},{7,23},{8,24},{9,... | collective-permute-start | bytes 1572872 | tf_op jit(solution)/shard_map/ppermute | solution.py:30
  11.8 3.4 %collective-permute-start.10 = (bf16[128,2048]{1,0:T(8,128)(2,1)S(1)}, bf16[128,2048]{1,0:T(8,128)(2,1)S(1)}, u32[]{:S(2)}, u32[]{:S(2)}) collective-permute-start(bf16[128,2048]{1,0:T(8,128)(2,1)S(1)} %collective-permute-done.1.refs_2_), channel_id=1, source_target_pairs={{0,1},{1,0},{2,6},{3,7},{4,5},{5,4},{6,2},{7,3},{8,9},{9,8},{10,14... | collective-permute-start | bytes 1572872 | tf_op jit(solution)/shard_map/ppermute | solution.py:30
  17.1 7.9 %all-to-all-start = ((f32[16,2,2,128]{3,2,1,0:T(2,128)}), f32[16,2,2,128]{3,2,1,0:T(2,128)S(1)}, u32[]{:S(2)}, u32[]{:S(2)}) async-start(f32[16,2,2,128]{3,2,1,0:T(2,128)} %copy.12), calls=%async_computation | async-start | bytes 65536 | tf_op jit(solution)/shard_map/all_to_all | solution.py:318
  25.0 2.6 %collective-permute-done.4.refs_4_ = bf16[128,2048]{1,0:T(8,128)(2,1)S(1)} collective-permute-done((bf16[128,2048]{1,0:T(8,128)(2,1)}, bf16[128,2048]{1,0:T(8,128)(2,1)S(1)}, u32[]{:S(2)}, u32[]{:S(2)}) %collective-permute-start.4) | collective-permute-done | bytes 524320 | tf_op jit(solution)/shard_map/ppermute | solution.py:30
  27.7 2.6 %collective-permute-done.2.refs_4_ = bf16[128,2048]{1,0:T(8,128)(2,1)S(1)} collective-permute-done((bf16[128,2048]{1,0:T(8,128)(2,1)}, bf16[128,2048]{1,0:T(8,128)(2,1)S(1)}, u32[]{:S(2)}, u32[]{:S(2)}) %collective-permute-start.2) | collective-permute-done | bytes 524320 | tf_op jit(solution)/shard_map/ppermute | solution.py:30
  34.7 9.4 %collective-permute-done.7.refs_6_ = bf16[128,2048]{1,0:T(8,128)(2,1)S(1)} collective-permute-done((bf16[128,2048]{1,0:T(8,128)(2,1)S(1)}, bf16[128,2048]{1,0:T(8,128)(2,1)S(1)}, u32[]{:S(2)}, u32[]{:S(2)}) %collective-permute-start.7) | collective-permute-done | bytes 524320 | tf_op jit(solution)/shard_map/ppermute | solution.py:30
  48.8 7.1 %collective-permute-done.5.refs_6_ = bf16[128,2048]{1,0:T(8,128)(2,1)S(1)} collective-permute-done((bf16[128,2048]{1,0:T(8,128)(2,1)S(1)}, bf16[128,2048]{1,0:T(8,128)(2,1)S(1)}, u32[]{:S(2)}, u32[]{:S(2)}) %collective-permute-start.5) | collective-permute-done | bytes 524320 | tf_op jit(solution)/shard_map/ppermute | solution.py:30
  58.1 3.3 %collective-permute-done.3.refs_0_ = bf16[128,2048]{1,0:T(8,128)(2,1)S(1)} collective-permute-done((bf16[128,2048]{1,0:T(8,128)(2,1)S(1)}, bf16[128,2048]{1,0:T(8,128)(2,1)S(1)}, u32[]{:S(2)}, u32[]{:S(2)}) %collective-permute-start.3) | collective-permute-done | bytes 524320 | tf_op jit(solution)/shard_map/ppermute | solution.py:30
  61.4 3.7 %collective-permute-done.6.refs_7_ = bf16[128,2048]{1,0:T(8,128)(2,1)S(1)} collective-permute-done((bf16[128,2048]{1,0:T(8,128)(2,1)S(1)}, bf16[128,2048]{1,0:T(8,128)(2,1)S(1)}, u32[]{:S(2)}, u32[]{:S(2)}) %collective-permute-start.6) | collective-permute-done | bytes 524320 | tf_op jit(solution)/shard_map/ppermute | solution.py:30
  67.8 16.4 %hidden_units.2.refs_2_ = bf16[2,384,768]{2,1,0:T(8,128)(2,1)S(1)} custom-call(bf16[128,2048]{1,0:T(8,128)(2,1)S(1)} %copy-done.1, bf16[128,2048]{1,0:T(8,128)(2,1)S(1)} %collective-permute-done.refs_1_, bf16[128,2048]{1,0:T(8,128)(2,1)S(1)} %collective-permute-done.1.refs_2_, bf16[128,2048]{1,0:T(8,128)(2,1)S(1)} %collective-permute-done.10.refs_3_, ...), custom_call_target="tpu_custom_call" | custom-call | flops 9663676416 | bytes 33554432 | tf_op jit(solution)/shard_map/hidden_units/pallas_call | solution.py:190
  86.0 3.3 %collective-permute-done.18.refs_9_ = bf16[4,128,2048]{2,1,0:T(8,128)(2,1)S(1)} collective-permute-done((bf16[4,128,2048]{2,1,0:T(8,128)(2,1)S(1)}, bf16[4,128,2048]{2,1,0:T(8,128)(2,1)S(1)}, u32[]{:S(2)}, u32[]{:S(2)}) %collective-permute-start.18) | collective-permute-done | bytes 2097184 | tf_op jit(solution)/shard_map/ppermute | solution.py:30
  89.3 3.0 %collective-permute-done.17.refs_8_ = bf16[4,128,2048]{2,1,0:T(8,128)(2,1)S(1)} collective-permute-done((bf16[4,128,2048]{2,1,0:T(8,128)(2,1)S(1)}, bf16[4,128,2048]{2,1,0:T(8,128)(2,1)S(1)}, u32[]{:S(2)}, u32[]{:S(2)}) %collective-permute-start.17) | collective-permute-done | bytes 2097184 | tf_op jit(solution)/shard_map/ppermute | solution.py:30
  92.3 16.4 %hidden_units.3.refs_2_ = bf16[2,384,768]{2,1,0:T(8,128)(2,1)S(1)} custom-call(bf16[128,2048]{1,0:T(8,128)(2,1)S(1)} %collective-permute-done.3.refs_0_, bf16[128,2048]{1,0:T(8,128)(2,1)S(1)} %collective-permute-done.8.refs_1_, bf16[128,2048]{1,0:T(8,128)(2,1)S(1)} %collective-permute-done.9.refs_2_, bf16[128,2048]{1,0:T(8,128)(2,1)S(1)} %collective-permute-done.12.refs_3_, ...), custom_call_target="tpu_custom_call" | custom-call | flops 9663676416 | bytes 33554432 | tf_op jit(solution)/shard_map/hidden_units/pallas_call | solution.py:190
  108.7 12.3 %weighted_outputs.2 = (bf16[4,2,128,2048]{3,2,1,0:T(8,128)(2,1)S(1)}, bf16[2,2,128,2048]{3,2,1,0:T(8,128)(2,1)}, bf16[2,2,128,2048]{3,2,1,0:T(8,128)(2,1)S(1)}) custom-call(f32[16,128]{1,0:T(8,128)S(1)} %bitcast.121, f32[16,128]{1,0:T(8,128)S(1)} %bitcast.122, bf16[2,384,768]{2,1,0:T(8,128)(2,1)S(1)} %hidden_units.3.refs_2_, bf16[2,768,4096]{2,1,0:T(8,128)(2,1)} %refs_3_.3), custom_call_target="tpu_custom_call" | custom-call | flops 38654705664 | bytes 20971520 | tf_op jit(solution)/shard_map/weighted_outputs/pallas_call | solution.py:225
  123.5 2.5 %fusion.33 = (bf16[2,2,128,2048]{3,2,1,0:T(8,128)(2,1)S(1)}, bf16[2,2,128,2048]{3,2,1,0:T(8,128)(2,1)S(1)}) fusion(bf16[4,2,128,2048]{3,2,1,0:T(8,128)(2,1)} %copy-done), kind=kLoop, calls=%fused_computation.77 | loop fusion | bytes 8388608 | tf_op jit(solution)/shard_map/slice | solution.py:346
  126.1 3.1 %collective-permute-done.19 = bf16[2,2,128,2048]{3,2,1,0:T(8,128)(2,1)} collective-permute-done((bf16[2,2,128,2048]{3,2,1,0:T(8,128)(2,1)}, bf16[2,2,128,2048]{3,2,1,0:T(8,128)(2,1)}, u32[]{:S(2)}, u32[]{:S(2)}) %collective-permute-start.19) | collective-permute-done | bytes 2097184 | tf_op jit(solution)/shard_map/ppermute | solution.py:30
  134.7 11.8 %weighted_outputs.3 = (bf16[4,2,128,2048]{3,2,1,0:T(8,128)(2,1)S(1)}, bf16[2,2,128,2048]{3,2,1,0:T(8,128)(2,1)S(1)}, bf16[2,2,128,2048]{3,2,1,0:T(8,128)(2,1)S(1)}) custom-call(f32[16,128]{1,0:T(8,128)S(1)} %bitcast.119, f32[16,128]{1,0:T(8,128)S(1)} %bitcast.117, bf16[2,384,768]{2,1,0:T(8,128)(2,1)S(1)} %copy-done.3, bf16[2,768,4096]{2,1,0:T(8,128)(2,1)} %refs_3_.3), custom_call_target="tpu_custom_call" | custom-call | flops 38654705664 | bytes 20971520 | tf_op jit(solution)/shard_map/weighted_outputs/pallas_call | solution.py:225
  151.1 5.0 %collective-permute-done.24 = bf16[128,2048]{1,0:T(8,128)(2,1)S(1)} collective-permute-done((bf16[128,2048]{1,0:T(8,128)(2,1)S(1)}, bf16[128,2048]{1,0:T(8,128)(2,1)S(1)}, u32[]{:S(2)}, u32[]{:S(2)}) %collective-permute-start.24) | collective-permute-done | bytes 524320 | tf_op jit(solution)/shard_map/ppermute | solution.py:30
  159.4 5.3 %collective-permute-done.22 = bf16[128,2048]{1,0:T(8,128)(2,1)S(1)} collective-permute-done((bf16[128,2048]{1,0:T(8,128)(2,1)S(1)}, bf16[128,2048]{1,0:T(8,128)(2,1)S(1)}, u32[]{:S(2)}, u32[]{:S(2)}) %collective-permute-start.22) | collective-permute-done | bytes 524320 | tf_op jit(solution)/shard_map/ppermute | solution.py:30
  170.7 11.3 %collective-permute-done.35 = bf16[128,2048]{1,0:T(8,128)(2,1)S(1)} collective-permute-done((bf16[128,2048]{1,0:T(8,128)(2,1)S(1)}, bf16[128,2048]{1,0:T(8,128)(2,1)S(1)}, u32[]{:S(2)}, u32[]{:S(2)}) %collective-permute-start.35) | collective-permute-done | bytes 524320 | tf_op jit(solution)/shard_map/ppermute | solution.py:30
  185.7 5.8 %collective-permute-done.36 = bf16[128,2048]{1,0:T(8,128)(2,1)S(1)} collective-permute-done((bf16[128,2048]{1,0:T(8,128)(2,1)S(1)}, bf16[128,2048]{1,0:T(8,128)(2,1)S(1)}, u32[]{:S(2)}, u32[]{:S(2)}) %collective-permute-start.36) | collective-permute-done | bytes 524320 | tf_op jit(solution)/shard_map/ppermute | solution.py:30
  194.1 6.9 %collective-permute-done.34 = bf16[128,2048]{1,0:T(8,128)(2,1)S(1)} collective-permute-done((bf16[128,2048]{1,0:T(8,128)(2,1)S(1)}, bf16[128,2048]{1,0:T(8,128)(2,1)S(1)}, u32[]{:S(2)}, u32[]{:S(2)}) %collective-permute-start.34) | collective-permute-done | bytes 524320 | tf_op jit(solution)/shard_map/ppermute | solution.py:30
  200.9 2.6 %collective-permute-done.33 = bf16[128,2048]{1,0:T(8,128)(2,1)S(1)} collective-permute-done((bf16[128,2048]{1,0:T(8,128)(2,1)S(1)}, bf16[128,2048]{1,0:T(8,128)(2,1)S(1)}, u32[]{:S(2)}, u32[]{:S(2)}) %collective-permute-start.33) | collective-permute-done | bytes 524320 | tf_op jit(solution)/shard_map/ppermute | solution.py:30
  (102 shorter events, 53.4 us)
Async XLA Ops:
  2.9 24.7 %collective-permute-start.4 = (bf16[128,2048]{1,0:T(8,128)(2,1)}, bf16[128,2048]{1,0:T(8,128)(2,1)S(1)}, u32[]{:S(2)}, u32[]{:S(2)}) collective-permute-start(bf16[128,2048]{1,0:T(8,128)(2,1)} %refs_0_.1), channel_id=1, source_target_pairs={{0,8},{1,9},{2,10},{3,11},{4,12},{5,13},{6,14},{7,15},{8,0},{9,1},... | collective-permute-start | bytes 1572872 | tf_op jit(solution)/shard_map/ppermute | solution.py:30
  4.5 25.8 %collective-permute-start.2 = (bf16[128,2048]{1,0:T(8,128)(2,1)}, bf16[128,2048]{1,0:T(8,128)(2,1)S(1)}, u32[]{:S(2)}, u32[]{:S(2)}) collective-permute-start(bf16[128,2048]{1,0:T(8,128)(2,1)} %refs_0_.1), channel_id=1, source_target_pairs={{0,16},{1,17},{2,18},{3,19},{4,20},{5,21},{6,22},{7,23},{8,24},{9,... | collective-permute-start | bytes 1572872 | tf_op jit(solution)/shard_map/ppermute | solution.py:30
  11.8 21.2 %collective-permute-start.10 = (bf16[128,2048]{1,0:T(8,128)(2,1)S(1)}, bf16[128,2048]{1,0:T(8,128)(2,1)S(1)}, u32[]{:S(2)}, u32[]{:S(2)}) collective-permute-start(bf16[128,2048]{1,0:T(8,128)(2,1)S(1)} %collective-permute-done.1.refs_2_), channel_id=1, source_target_pairs={{0,1},{1,0},{2,6},{3,7},{4,5},{5,4},{6,2},{7,3},{8,9},{9,8},{10,14... | collective-permute-start | bytes 1572872 | tf_op jit(solution)/shard_map/ppermute | solution.py:30
  17.1 14.7 %all-to-all-start = ((f32[16,2,2,128]{3,2,1,0:T(2,128)}), f32[16,2,2,128]{3,2,1,0:T(2,128)S(1)}, u32[]{:S(2)}, u32[]{:S(2)}) async-start(f32[16,2,2,128]{3,2,1,0:T(2,128)} %copy.12), calls=%async_computation | async-start | bytes 65536 | tf_op jit(solution)/shard_map/all_to_all | solution.py:318
  30.3 13.8 %collective-permute-start.7 = (bf16[128,2048]{1,0:T(8,128)(2,1)S(1)}, bf16[128,2048]{1,0:T(8,128)(2,1)S(1)}, u32[]{:S(2)}, u32[]{:S(2)}) collective-permute-start(bf16[128,2048]{1,0:T(8,128)(2,1)S(1)} %collective-permute-done.4.refs_4_), channel_id=1, source_target_pairs={{0,4},{1,5},{2,3},{3,2},{4,0},{5,1},{6,7},{7,6},{8,12},{9,13},{10,... | collective-permute-start | bytes 1572872 | tf_op jit(solution)/shard_map/ppermute | solution.py:30
  34.6 32.5 %collective-permute-start.15 = (bf16[4,128,2048]{2,1,0:T(8,128)(2,1)S(1)}, bf16[4,128,2048]{2,1,0:T(8,128)(2,1)S(1)}, u32[]{:S(2)}, u32[]{:S(2)}) collective-permute-start(bf16[4,128,2048]{2,1,0:T(8,128)(2,1)S(1)} %pad_maximum_fusion), channel_id=1, source_target_pairs={{0,2},{1,3},{2,0},{3,1},{4,6},{5,7},{6,4},{7,5},{8,10},{9,11},{10,... | collective-permute-start | bytes 6291464 | tf_op jit(solution)/shard_map/ppermute | solution.py:30
  46.6 21.2 %collective-permute-start.16 = (bf16[4,128,2048]{2,1,0:T(8,128)(2,1)S(1)}, bf16[4,128,2048]{2,1,0:T(8,128)(2,1)S(1)}, u32[]{:S(2)}, u32[]{:S(2)}) collective-permute-start(bf16[4,128,2048]{2,1,0:T(8,128)(2,1)S(1)} %pad_maximum_fusion.1), channel_id=1, source_target_pairs={{0,2},{1,3},{2,0},{3,1},{4,6},{5,7},{6,4},{7,5},{8,10},{9,11},{10,... | collective-permute-start | bytes 6291464 | tf_op jit(solution)/shard_map/ppermute | solution.py:30
  56.6 27.6 %collective-permute-start.14 = (bf16[128,2048]{1,0:T(8,128)(2,1)S(1)}, bf16[128,2048]{1,0:T(8,128)(2,1)S(1)}, u32[]{:S(2)}, u32[]{:S(2)}) collective-permute-start(bf16[128,2048]{1,0:T(8,128)(2,1)S(1)} %collective-permute-done.2.refs_4_), channel_id=1, source_target_pairs={{0,1},{1,0},{2,6},{3,7},{4,5},{5,4},{6,2},{7,3},{8,9},{9,8},{10,14... | collective-permute-start | bytes 1572872 | tf_op jit(solution)/shard_map/ppermute | solution.py:30
  65.1 19.1 %collective-permute-start.9 = (bf16[128,2048]{1,0:T(8,128)(2,1)S(1)}, bf16[128,2048]{1,0:T(8,128)(2,1)S(1)}, u32[]{:S(2)}, u32[]{:S(2)}) collective-permute-start(bf16[128,2048]{1,0:T(8,128)(2,1)S(1)} %collective-permute-done.3.refs_0_), channel_id=1, source_target_pairs={{0,4},{1,5},{2,3},{3,2},{4,0},{5,1},{6,7},{7,6},{8,12},{9,13},{10,... | collective-permute-start | bytes 1572872 | tf_op jit(solution)/shard_map/ppermute | solution.py:30
  66.6 17.6 %collective-permute-start.8 = (bf16[128,2048]{1,0:T(8,128)(2,1)S(1)}, bf16[128,2048]{1,0:T(8,128)(2,1)S(1)}, u32[]{:S(2)}, u32[]{:S(2)}) collective-permute-start(bf16[128,2048]{1,0:T(8,128)(2,1)S(1)} %collective-permute-done.3.refs_0_), channel_id=1, source_target_pairs={{0,1},{1,0},{2,6},{3,7},{4,5},{5,4},{6,2},{7,3},{8,9},{9,8},{10,14... | collective-permute-start | bytes 1572872 | tf_op jit(solution)/shard_map/ppermute | solution.py:30
  67.1 17.1 %collective-permute-start.12 = (bf16[128,2048]{1,0:T(8,128)(2,1)S(1)}, bf16[128,2048]{1,0:T(8,128)(2,1)S(1)}, u32[]{:S(2)}, u32[]{:S(2)}) collective-permute-start(bf16[128,2048]{1,0:T(8,128)(2,1)S(1)} %collective-permute-done.6.refs_7_), channel_id=1, source_target_pairs={{0,8},{1,9},{2,10},{3,11},{4,12},{5,13},{6,14},{7,15},{8,0},{9,1},... | collective-permute-start | bytes 1572872 | tf_op jit(solution)/shard_map/ppermute | solution.py:30
  123.2 23.4 %collective-permute-start.21 = (bf16[2,2,128,2048]{3,2,1,0:T(8,128)(2,1)S(1)}, bf16[2,2,128,2048]{3,2,1,0:T(8,128)(2,1)S(1)}, u32[]{:S(2)}, u32[]{:S(2)}) collective-permute-start(bf16[2,2,128,2048]{3,2,1,0:T(8,128)(2,1)S(1)} %get-tuple-element.47), channel_id=1, source_target_pairs={{0,2},{1,3},{2,0},{3,1},{4,6},{5,7},{6,4},{7,5},{8,10},{9,11},{10,... | collective-permute-start | bytes 6291464 | tf_op jit(solution)/shard_map/ppermute | solution.py:30
  131.2 15.4 %collective-permute-start.23 = (bf16[128,2048]{1,0:T(8,128)(2,1)S(1)}, bf16[128,2048]{1,0:T(8,128)(2,1)S(1)}, u32[]{:S(2)}, u32[]{:S(2)}) collective-permute-start(bf16[128,2048]{1,0:T(8,128)(2,1)S(1)} %get-tuple-element.53), channel_id=1, source_target_pairs={{0,8},{1,9},{2,10},{3,11},{4,12},{5,13},{6,14},{7,15},{8,0},{9,1},... | collective-permute-start | bytes 1572872 | tf_op jit(solution)/shard_map/ppermute | solution.py:30
  132.5 16.6 %collective-permute-start.27 = (bf16[128,2048]{1,0:T(8,128)(2,1)S(1)}, bf16[128,2048]{1,0:T(8,128)(2,1)S(1)}, u32[]{:S(2)}, u32[]{:S(2)}) collective-permute-start(bf16[128,2048]{1,0:T(8,128)(2,1)S(1)} %get-tuple-element.54), channel_id=1, source_target_pairs={{0,4},{1,5},{2,3},{3,2},{4,0},{5,1},{6,7},{7,6},{8,12},{9,13},{10,... | collective-permute-start | bytes 1572872 | tf_op jit(solution)/shard_map/ppermute | solution.py:30
  133.4 15.8 %collective-permute-start.26 = (bf16[128,2048]{1,0:T(8,128)(2,1)S(1)}, bf16[128,2048]{1,0:T(8,128)(2,1)S(1)}, u32[]{:S(2)}, u32[]{:S(2)}) collective-permute-start(bf16[128,2048]{1,0:T(8,128)(2,1)S(1)} %get-tuple-element.55), channel_id=1, source_target_pairs={{0,1},{1,0},{2,6},{3,7},{4,5},{5,4},{6,2},{7,3},{8,9},{9,8},{10,14... | collective-permute-start | bytes 1572872 | tf_op jit(solution)/shard_map/ppermute | solution.py:30
  147.7 17.0 %collective-permute-start.22 = (bf16[128,2048]{1,0:T(8,128)(2,1)S(1)}, bf16[128,2048]{1,0:T(8,128)(2,1)S(1)}, u32[]{:S(2)}, u32[]{:S(2)}) collective-permute-start(bf16[128,2048]{1,0:T(8,128)(2,1)S(1)} %fusion.16), channel_id=1, source_target_pairs={{0,1},{1,0},{2,6},{3,7},{4,5},{5,4},{6,2},{7,3},{8,9},{9,8},{10,14... | collective-permute-start | bytes 1572872 | tf_op jit(solution)/shard_map/ppermute | solution.py:30
  149.1 21.6 %collective-permute-start.20 = (bf16[2,2,128,2048]{3,2,1,0:T(8,128)(2,1)S(1)}, bf16[2,2,128,2048]{3,2,1,0:T(8,128)(2,1)S(1)}, u32[]{:S(2)}, u32[]{:S(2)}) collective-permute-start(bf16[2,2,128,2048]{3,2,1,0:T(8,128)(2,1)S(1)} %get-tuple-element.45), channel_id=1, source_target_pairs={{0,2},{1,3},{2,0},{3,1},{4,6},{5,7},{6,4},{7,5},{8,10},{9,11},{10,... | collective-permute-start | bytes 6291464 | tf_op jit(solution)/shard_map/ppermute | solution.py:30
  150.5 14.8 %collective-permute-start.28 = (bf16[128,2048]{1,0:T(8,128)(2,1)S(1)}, bf16[128,2048]{1,0:T(8,128)(2,1)S(1)}, u32[]{:S(2)}, u32[]{:S(2)}) collective-permute-start(bf16[128,2048]{1,0:T(8,128)(2,1)S(1)} %fusion.6), channel_id=1, source_target_pairs={{0,8},{1,9},{2,10},{3,11},{4,12},{5,13},{6,14},{7,15},{8,0},{9,1},... | collective-permute-start | bytes 1572872 | tf_op jit(solution)/shard_map/ppermute | solution.py:30
  158.7 23.3 %collective-permute-start.35 = (bf16[128,2048]{1,0:T(8,128)(2,1)S(1)}, bf16[128,2048]{1,0:T(8,128)(2,1)S(1)}, u32[]{:S(2)}, u32[]{:S(2)}) collective-permute-start(bf16[128,2048]{1,0:T(8,128)(2,1)S(1)} %get-tuple-element.57), channel_id=1, source_target_pairs={{0,8},{1,9},{2,10},{3,11},{4,12},{5,13},{6,14},{7,15},{8,0},{9,1},... | collective-permute-start | bytes 1572872 | tf_op jit(solution)/shard_map/ppermute | solution.py:30
  167.3 26.8 %collective-permute-start.29 = (bf16[128,2048]{1,0:T(8,128)(2,1)S(1)}, bf16[128,2048]{1,0:T(8,128)(2,1)S(1)}, u32[]{:S(2)}, u32[]{:S(2)}) collective-permute-start(bf16[128,2048]{1,0:T(8,128)(2,1)S(1)} %fusion.11), channel_id=1, source_target_pairs={{0,16},{1,17},{2,18},{3,19},{4,20},{5,21},{6,22},{7,23},{8,24},{9,... | collective-permute-start | bytes 1572872 | tf_op jit(solution)/shard_map/ppermute | solution.py:30
  169.0 15.6 %collective-permute-start.32 = (bf16[128,2048]{1,0:T(8,128)(2,1)S(1)}, bf16[128,2048]{1,0:T(8,128)(2,1)S(1)}, u32[]{:S(2)}, u32[]{:S(2)}) collective-permute-start(bf16[128,2048]{1,0:T(8,128)(2,1)S(1)} %get-tuple-element.50), channel_id=1, source_target_pairs={{0,4},{1,5},{2,3},{3,2},{4,0},{5,1},{6,7},{7,6},{8,12},{9,13},{10,... | collective-permute-start | bytes 1572872 | tf_op jit(solution)/shard_map/ppermute | solution.py:30
  170.2 14.3 %collective-permute-start.31 = (bf16[128,2048]{1,0:T(8,128)(2,1)S(1)}, bf16[128,2048]{1,0:T(8,128)(2,1)S(1)}, u32[]{:S(2)}, u32[]{:S(2)}) collective-permute-start(bf16[128,2048]{1,0:T(8,128)(2,1)S(1)} %get-tuple-element.56), channel_id=1, source_target_pairs={{0,1},{1,0},{2,6},{3,7},{4,5},{5,4},{6,2},{7,3},{8,9},{9,8},{10,14... | collective-permute-start | bytes 1572872 | tf_op jit(solution)/shard_map/ppermute | solution.py:30
  183.5 17.5 %collective-permute-start.34 = (bf16[128,2048]{1,0:T(8,128)(2,1)S(1)}, bf16[128,2048]{1,0:T(8,128)(2,1)S(1)}, u32[]{:S(2)}, u32[]{:S(2)}) collective-permute-start(bf16[128,2048]{1,0:T(8,128)(2,1)S(1)} %fusion.22), channel_id=1, source_target_pairs={{0,1},{1,0},{2,6},{3,7},{4,5},{5,4},{6,2},{7,3},{8,9},{9,8},{10,14... | collective-permute-start | bytes 1572872 | tf_op jit(solution)/shard_map/ppermute | solution.py:30
  184.9 18.6 %collective-permute-start.33 = (bf16[128,2048]{1,0:T(8,128)(2,1)S(1)}, bf16[128,2048]{1,0:T(8,128)(2,1)S(1)}, u32[]{:S(2)}, u32[]{:S(2)}) collective-permute-start(bf16[128,2048]{1,0:T(8,128)(2,1)S(1)} %fusion.4), channel_id=1, source_target_pairs={{0,8},{1,9},{2,10},{3,11},{4,12},{5,13},{6,14},{7,15},{8,0},{9,1},... | collective-permute-start | bytes 1572872 | tf_op jit(solution)/shard_map/ppermute | solution.py:30
  (19 other events, 177.4 us)

commit v4 on v3

--- a/solution.py
+++ b/solution.py
@@ -216,7 +216,7 @@
 def run_outputs(hidden, pos, weight, w_down, slots, half):
     experts, hid, width = w_down.shape
     lines, rows = pos.shape
-    col_block = 512
+    col_block = 1024
     blocks = lines // experts
     groups = blocks // 4
     used = blocks * slots

time: 205 us -> 204 us (level)
  no operation moved by 1% of the time
where the time goes in v4:
time: 204 us
  waiting for transfers between devices  83.1 us (41%)
  Pallas kernels  55.8 us (27%)
  starting transfers between devices  46.7 us (23%)
  other arithmetic  10.9 us (5%)
  local copies, waits for them, and re-layouts  6.81 us (3%)
    ppermute x38, waiting for transfers between devices, hop(): return lax.ppermute(value, AXES, link_pairs(link))  83.1 us
    ppermute x38, starting transfers between devices, hop(): return lax.ppermute(value, AXES, link_pairs(link))  38.8 us
    pallas_call x2, Pallas kernels, run_hidden(): pl.pallas_call(functools.partial(hidden_kernel, slots, ring), out_shape=j...  32.7 us
    pallas_call x2, Pallas kernels, run_outputs(): pl.pallas_call(functools.partial(output_kernel, slots, groups), out_shape...  23.1 us
    all_to_all x1, starting transfers between devices, tables_after(): lax.all_to_all(own.reshape(dp_count, experts, 2, rows), 'dp', split_axis=...  7.88 us
    convert_element_type x12, other arithmetic, total(): return sum((t.astype(F32) for t in terms)).astype(BF16)  7.32 us
  transfers between devices with their start and end apart: 39, of which 21 were waited for; matrix products, arithmetic and copies ran while one was open for 7% of the time, Pallas kernels for 14%

profile of v4, /device:TPU:0, one launch (start us, length us, event | category | flops | bytes accessed | tf_op | source)
XLA Modules:
  0.0 203.9 jit_solution(4888516228376150343)
XLA Ops:
  0.0 2.9 %collective-permute-start.1 = (bf16[128,2048]{1,0:T(8,128)(2,1)}, bf16[128,2048]{1,0:T(8,128)(2,1)S(1)}, u32[]{:S(2)}, u32[]{:S(2)}) collective-permute-start(bf16[128,2048]{1,0:T(8,128)(2,1)} %refs_0_.1), channel_id=1, source_target_pairs={{0,4},{1,5},{2,3},{3,2},{4,0},{5,1},{6,7},{7,6},{8,12},{9,13},{10,... | collective-permute-start | bytes 1572872 | tf_op jit(solution)/shard_map/ppermute | solution.py:30
  4.5 2.6 %collective-permute-start.2 = (bf16[128,2048]{1,0:T(8,128)(2,1)}, bf16[128,2048]{1,0:T(8,128)(2,1)S(1)}, u32[]{:S(2)}, u32[]{:S(2)}) collective-permute-start(bf16[128,2048]{1,0:T(8,128)(2,1)} %refs_0_.1), channel_id=1, source_target_pairs={{0,16},{1,17},{2,18},{3,19},{4,20},{5,21},{6,22},{7,23},{8,24},{9,... | collective-permute-start | bytes 1572872 | tf_op jit(solution)/shard_map/ppermute | solution.py:30
  11.8 3.4 %collective-permute-start.10 = (bf16[128,2048]{1,0:T(8,128)(2,1)S(1)}, bf16[128,2048]{1,0:T(8,128)(2,1)S(1)}, u32[]{:S(2)}, u32[]{:S(2)}) collective-permute-start(bf16[128,2048]{1,0:T(8,128)(2,1)S(1)} %collective-permute-done.1.refs_2_), channel_id=1, source_target_pairs={{0,1},{1,0},{2,6},{3,7},{4,5},{5,4},{6,2},{7,3},{8,9},{9,8},{10,14... | collective-permute-start | bytes 1572872 | tf_op jit(solution)/shard_map/ppermute | solution.py:30
  17.1 7.9 %all-to-all-start = ((f32[16,2,2,128]{3,2,1,0:T(2,128)}), f32[16,2,2,128]{3,2,1,0:T(2,128)S(1)}, u32[]{:S(2)}, u32[]{:S(2)}) async-start(f32[16,2,2,128]{3,2,1,0:T(2,128)} %copy.12), calls=%async_computation | async-start | bytes 65536 | tf_op jit(solution)/shard_map/all_to_all | solution.py:318
  25.0 2.6 %collective-permute-done.4.refs_4_ = bf16[128,2048]{1,0:T(8,128)(2,1)S(1)} collective-permute-done((bf16[128,2048]{1,0:T(8,128)(2,1)}, bf16[128,2048]{1,0:T(8,128)(2,1)S(1)}, u32[]{:S(2)}, u32[]{:S(2)}) %collective-permute-start.4) | collective-permute-done | bytes 524320 | tf_op jit(solution)/shard_map/ppermute | solution.py:30
  27.7 2.6 %collective-permute-done.2.refs_4_ = bf16[128,2048]{1,0:T(8,128)(2,1)S(1)} collective-permute-done((bf16[128,2048]{1,0:T(8,128)(2,1)}, bf16[128,2048]{1,0:T(8,128)(2,1)S(1)}, u32[]{:S(2)}, u32[]{:S(2)}) %collective-permute-start.2) | collective-permute-done | bytes 524320 | tf_op jit(solution)/shard_map/ppermute | solution.py:30
  34.7 9.4 %collective-permute-done.7.refs_6_ = bf16[128,2048]{1,0:T(8,128)(2,1)S(1)} collective-permute-done((bf16[128,2048]{1,0:T(8,128)(2,1)S(1)}, bf16[128,2048]{1,0:T(8,128)(2,1)S(1)}, u32[]{:S(2)}, u32[]{:S(2)}) %collective-permute-start.7) | collective-permute-done | bytes 524320 | tf_op jit(solution)/shard_map/ppermute | solution.py:30
  48.8 7.1 %collective-permute-done.5.refs_6_ = bf16[128,2048]{1,0:T(8,128)(2,1)S(1)} collective-permute-done((bf16[128,2048]{1,0:T(8,128)(2,1)S(1)}, bf16[128,2048]{1,0:T(8,128)(2,1)S(1)}, u32[]{:S(2)}, u32[]{:S(2)}) %collective-permute-start.5) | collective-permute-done | bytes 524320 | tf_op jit(solution)/shard_map/ppermute | solution.py:30
  58.1 3.3 %collective-permute-done.3.refs_0_ = bf16[128,2048]{1,0:T(8,128)(2,1)S(1)} collective-permute-done((bf16[128,2048]{1,0:T(8,128)(2,1)S(1)}, bf16[128,2048]{1,0:T(8,128)(2,1)S(1)}, u32[]{:S(2)}, u32[]{:S(2)}) %collective-permute-start.3) | collective-permute-done | bytes 524320 | tf_op jit(solution)/shard_map/ppermute | solution.py:30
  61.4 3.7 %collective-permute-done.6.refs_7_ = bf16[128,2048]{1,0:T(8,128)(2,1)S(1)} collective-permute-done((bf16[128,2048]{1,0:T(8,128)(2,1)S(1)}, bf16[128,2048]{1,0:T(8,128)(2,1)S(1)}, u32[]{:S(2)}, u32[]{:S(2)}) %collective-permute-start.6) | collective-permute-done | bytes 524320 | tf_op jit(solution)/shard_map/ppermute | solution.py:30
  67.8 16.4 %hidden_units.2.refs_2_ = bf16[2,384,768]{2,1,0:T(8,128)(2,1)S(1)} custom-call(bf16[128,2048]{1,0:T(8,128)(2,1)S(1)} %copy-done.1, bf16[128,2048]{1,0:T(8,128)(2,1)S(1)} %collective-permute-done.refs_1_, bf16[128,2048]{1,0:T(8,128)(2,1)S(1)} %collective-permute-done.1.refs_2_, bf16[128,2048]{1,0:T(8,128)(2,1)S(1)} %collective-permute-done.10.refs_3_, ...), custom_call_target="tpu_custom_call" | custom-call | flops 9663676416 | bytes 33554432 | tf_op jit(solution)/shard_map/hidden_units/pallas_call | solution.py:190
  86.0 3.3 %collective-permute-done.18.refs_9_ = bf16[4,128,2048]{2,1,0:T(8,128)(2,1)S(1)} collective-permute-done((bf16[4,128,2048]{2,1,0:T(8,128)(2,1)S(1)}, bf16[4,128,2048]{2,1,0:T(8,128)(2,1)S(1)}, u32[]{:S(2)}, u32[]{:S(2)}) %collective-permute-start.18) | collective-permute-done | bytes 2097184 | tf_op jit(solution)/shard_map/ppermute | solution.py:30
  89.3 3.0 %collective-permute-done.17.refs_8_ = bf16[4,128,2048]{2,1,0:T(8,128)(2,1)S(1)} collective-permute-done((bf16[4,128,2048]{2,1,0:T(8,128)(2,1)S(1)}, bf16[4,128,2048]{2,1,0:T(8,128)(2,1)S(1)}, u32[]{:S(2)}, u32[]{:S(2)}) %collective-permute-start.17) | collective-permute-done | bytes 2097184 | tf_op jit(solution)/shard_map/ppermute | solution.py:30
  92.3 16.4 %hidden_units.3.refs_2_ = bf16[2,384,768]{2,1,0:T(8,128)(2,1)S(1)} custom-call(bf16[128,2048]{1,0:T(8,128)(2,1)S(1)} %collective-permute-done.3.refs_0_, bf16[128,2048]{1,0:T(8,128)(2,1)S(1)} %collective-permute-done.8.refs_1_, bf16[128,2048]{1,0:T(8,128)(2,1)S(1)} %collective-permute-done.9.refs_2_, bf16[128,2048]{1,0:T(8,128)(2,1)S(1)} %collective-permute-done.12.refs_3_, ...), custom_call_target="tpu_custom_call" | custom-call | flops 9663676416 | bytes 33554432 | tf_op jit(solution)/shard_map/hidden_units/pallas_call | solution.py:190
  108.7 11.9 %weighted_outputs.2 = (bf16[4,2,128,2048]{3,2,1,0:T(8,128)(2,1)S(1)}, bf16[2,2,128,2048]{3,2,1,0:T(8,128)(2,1)}, bf16[2,2,128,2048]{3,2,1,0:T(8,128)(2,1)S(1)}) custom-call(f32[16,128]{1,0:T(8,128)S(1)} %bitcast.121, f32[16,128]{1,0:T(8,128)S(1)} %bitcast.122, bf16[2,384,768]{2,1,0:T(8,128)(2,1)S(1)} %hidden_units.3.refs_2_, bf16[2,768,4096]{2,1,0:T(8,128)(2,1)} %refs_3_.3), custom_call_target="tpu_custom_call" | custom-call | flops 38654705664 | bytes 20971520 | tf_op jit(solution)/shard_map/weighted_outputs/pallas_call | solution.py:225
  123.1 2.5 %fusion.33 = (bf16[2,2,128,2048]{3,2,1,0:T(8,128)(2,1)S(1)}, bf16[2,2,128,2048]{3,2,1,0:T(8,128)(2,1)S(1)}) fusion(bf16[4,2,128,2048]{3,2,1,0:T(8,128)(2,1)} %copy-done), kind=kLoop, calls=%fused_computation.77 | loop fusion | bytes 8388608 | tf_op jit(solution)/shard_map/slice | solution.py:346
  125.6 3.1 %collective-permute-done.19 = bf16[2,2,128,2048]{3,2,1,0:T(8,128)(2,1)} collective-permute-done((bf16[2,2,128,2048]{3,2,1,0:T(8,128)(2,1)}, bf16[2,2,128,2048]{3,2,1,0:T(8,128)(2,1)}, u32[]{:S(2)}, u32[]{:S(2)}) %collective-permute-start.19) | collective-permute-done | bytes 2097184 | tf_op jit(solution)/shard_map/ppermute | solution.py:30
  134.3 11.3 %weighted_outputs.3 = (bf16[4,2,128,2048]{3,2,1,0:T(8,128)(2,1)S(1)}, bf16[2,2,128,2048]{3,2,1,0:T(8,128)(2,1)S(1)}, bf16[2,2,128,2048]{3,2,1,0:T(8,128)(2,1)S(1)}) custom-call(f32[16,128]{1,0:T(8,128)S(1)} %bitcast.119, f32[16,128]{1,0:T(8,128)S(1)} %bitcast.117, bf16[2,384,768]{2,1,0:T(8,128)(2,1)S(1)} %copy-done.3, bf16[2,768,4096]{2,1,0:T(8,128)(2,1)} %refs_3_.3), custom_call_target="tpu_custom_call" | custom-call | flops 38654705664 | bytes 20971520 | tf_op jit(solution)/shard_map/weighted_outputs/pallas_call | solution.py:225
  150.1 5.0 %collective-permute-done.24 = bf16[128,2048]{1,0:T(8,128)(2,1)S(1)} collective-permute-done((bf16[128,2048]{1,0:T(8,128)(2,1)S(1)}, bf16[128,2048]{1,0:T(8,128)(2,1)S(1)}, u32[]{:S(2)}, u32[]{:S(2)}) %collective-permute-start.24) | collective-permute-done | bytes 524320 | tf_op jit(solution)/shard_map/ppermute | solution.py:30
  158.4 5.3 %collective-permute-done.22 = bf16[128,2048]{1,0:T(8,128)(2,1)S(1)} collective-permute-done((bf16[128,2048]{1,0:T(8,128)(2,1)S(1)}, bf16[128,2048]{1,0:T(8,128)(2,1)S(1)}, u32[]{:S(2)}, u32[]{:S(2)}) %collective-permute-start.22) | collective-permute-done | bytes 524320 | tf_op jit(solution)/shard_map/ppermute | solution.py:30
  169.8 11.3 %collective-permute-done.35 = bf16[128,2048]{1,0:T(8,128)(2,1)S(1)} collective-permute-done((bf16[128,2048]{1,0:T(8,128)(2,1)S(1)}, bf16[128,2048]{1,0:T(8,128)(2,1)S(1)}, u32[]{:S(2)}, u32[]{:S(2)}) %collective-permute-start.35) | collective-permute-done | bytes 524320 | tf_op jit(solution)/shard_map/ppermute | solution.py:30
  184.7 5.8 %collective-permute-done.36 = bf16[128,2048]{1,0:T(8,128)(2,1)S(1)} collective-permute-done((bf16[128,2048]{1,0:T(8,128)(2,1)S(1)}, bf16[128,2048]{1,0:T(8,128)(2,1)S(1)}, u32[]{:S(2)}, u32[]{:S(2)}) %collective-permute-start.36) | collective-permute-done | bytes 524320 | tf_op jit(solution)/shard_map/ppermute | solution.py:30
  193.1 6.9 %collective-permute-done.34 = bf16[128,2048]{1,0:T(8,128)(2,1)S(1)} collective-permute-done((bf16[128,2048]{1,0:T(8,128)(2,1)S(1)}, bf16[128,2048]{1,0:T(8,128)(2,1)S(1)}, u32[]{:S(2)}, u32[]{:S(2)}) %collective-permute-start.34) | collective-permute-done | bytes 524320 | tf_op jit(solution)/shard_map/ppermute | solution.py:30
  199.9 2.6 %collective-permute-done.33 = bf16[128,2048]{1,0:T(8,128)(2,1)S(1)} collective-permute-done((bf16[128,2048]{1,0:T(8,128)(2,1)S(1)}, bf16[128,2048]{1,0:T(8,128)(2,1)S(1)}, u32[]{:S(2)}, u32[]{:S(2)}) %collective-permute-start.33) | collective-permute-done | bytes 524320 | tf_op jit(solution)/shard_map/ppermute | solution.py:30
  (102 shorter events, 53.4 us)
Async XLA Ops:
  2.9 24.7 %collective-permute-start.4 = (bf16[128,2048]{1,0:T(8,128)(2,1)}, bf16[128,2048]{1,0:T(8,128)(2,1)S(1)}, u32[]{:S(2)}, u32[]{:S(2)}) collective-permute-start(bf16[128,2048]{1,0:T(8,128)(2,1)} %refs_0_.1), channel_id=1, source_target_pairs={{0,8},{1,9},{2,10},{3,11},{4,12},{5,13},{6,14},{7,15},{8,0},{9,1},... | collective-permute-start | bytes 1572872 | tf_op jit(solution)/shard_map/ppermute | solution.py:30
  4.5 25.8 %collective-permute-start.2 = (bf16[128,2048]{1,0:T(8,128)(2,1)}, bf16[128,2048]{1,0:T(8,128)(2,1)S(1)}, u32[]{:S(2)}, u32[]{:S(2)}) collective-permute-start(bf16[128,2048]{1,0:T(8,128)(2,1)} %refs_0_.1), channel_id=1, source_target_pairs={{0,16},{1,17},{2,18},{3,19},{4,20},{5,21},{6,22},{7,23},{8,24},{9,... | collective-permute-start | bytes 1572872 | tf_op jit(solution)/shard_map/ppermute | solution.py:30
  11.8 21.2 %collective-permute-start.10 = (bf16[128,2048]{1,0:T(8,128)(2,1)S(1)}, bf16[128,2048]{1,0:T(8,128)(2,1)S(1)}, u32[]{:S(2)}, u32[]{:S(2)}) collective-permute-start(bf16[128,2048]{1,0:T(8,128)(2,1)S(1)} %collective-permute-done.1.refs_2_), channel_id=1, source_target_pairs={{0,1},{1,0},{2,6},{3,7},{4,5},{5,4},{6,2},{7,3},{8,9},{9,8},{10,14... | collective-permute-start | bytes 1572872 | tf_op jit(solution)/shard_map/ppermute | solution.py:30
  17.1 14.7 %all-to-all-start = ((f32[16,2,2,128]{3,2,1,0:T(2,128)}), f32[16,2,2,128]{3,2,1,0:T(2,128)S(1)}, u32[]{:S(2)}, u32[]{:S(2)}) async-start(f32[16,2,2,128]{3,2,1,0:T(2,128)} %copy.12), calls=%async_computation | async-start | bytes 65536 | tf_op jit(solution)/shard_map/all_to_all | solution.py:318
  30.3 13.8 %collective-permute-start.7 = (bf16[128,2048]{1,0:T(8,128)(2,1)S(1)}, bf16[128,2048]{1,0:T(8,128)(2,1)S(1)}, u32[]{:S(2)}, u32[]{:S(2)}) collective-permute-start(bf16[128,2048]{1,0:T(8,128)(2,1)S(1)} %collective-permute-done.4.refs_4_), channel_id=1, source_target_pairs={{0,4},{1,5},{2,3},{3,2},{4,0},{5,1},{6,7},{7,6},{8,12},{9,13},{10,... | collective-permute-start | bytes 1572872 | tf_op jit(solution)/shard_map/ppermute | solution.py:30
  34.6 32.5 %collective-permute-start.15 = (bf16[4,128,2048]{2,1,0:T(8,128)(2,1)S(1)}, bf16[4,128,2048]{2,1,0:T(8,128)(2,1)S(1)}, u32[]{:S(2)}, u32[]{:S(2)}) collective-permute-start(bf16[4,128,2048]{2,1,0:T(8,128)(2,1)S(1)} %pad_maximum_fusion), channel_id=1, source_target_pairs={{0,2},{1,3},{2,0},{3,1},{4,6},{5,7},{6,4},{7,5},{8,10},{9,11},{10,... | collective-permute-start | bytes 6291464 | tf_op jit(solution)/shard_map/ppermute | solution.py:30
  46.6 21.2 %collective-permute-start.16 = (bf16[4,128,2048]{2,1,0:T(8,128)(2,1)S(1)}, bf16[4,128,2048]{2,1,0:T(8,128)(2,1)S(1)}, u32[]{:S(2)}, u32[]{:S(2)}) collective-permute-start(bf16[4,128,2048]{2,1,0:T(8,128)(2,1)S(1)} %pad_maximum_fusion.1), channel_id=1, source_target_pairs={{0,2},{1,3},{2,0},{3,1},{4,6},{5,7},{6,4},{7,5},{8,10},{9,11},{10,... | collective-permute-start | bytes 6291464 | tf_op jit(solution)/shard_map/ppermute | solution.py:30
  56.6 27.6 %collective-permute-start.14 = (bf16[128,2048]{1,0:T(8,128)(2,1)S(1)}, bf16[128,2048]{1,0:T(8,128)(2,1)S(1)}, u32[]{:S(2)}, u32[]{:S(2)}) collective-permute-start(bf16[128,2048]{1,0:T(8,128)(2,1)S(1)} %collective-permute-done.2.refs_4_), channel_id=1, source_target_pairs={{0,1},{1,0},{2,6},{3,7},{4,5},{5,4},{6,2},{7,3},{8,9},{9,8},{10,14... | collective-permute-start | bytes 1572872 | tf_op jit(solution)/shard_map/ppermute | solution.py:30
  65.1 19.1 %collective-permute-start.9 = (bf16[128,2048]{1,0:T(8,128)(2,1)S(1)}, bf16[128,2048]{1,0:T(8,128)(2,1)S(1)}, u32[]{:S(2)}, u32[]{:S(2)}) collective-permute-start(bf16[128,2048]{1,0:T(8,128)(2,1)S(1)} %collective-permute-done.3.refs_0_), channel_id=1, source_target_pairs={{0,4},{1,5},{2,3},{3,2},{4,0},{5,1},{6,7},{7,6},{8,12},{9,13},{10,... | collective-permute-start | bytes 1572872 | tf_op jit(solution)/shard_map/ppermute | solution.py:30
  66.6 17.6 %collective-permute-start.8 = (bf16[128,2048]{1,0:T(8,128)(2,1)S(1)}, bf16[128,2048]{1,0:T(8,128)(2,1)S(1)}, u32[]{:S(2)}, u32[]{:S(2)}) collective-permute-start(bf16[128,2048]{1,0:T(8,128)(2,1)S(1)} %collective-permute-done.3.refs_0_), channel_id=1, source_target_pairs={{0,1},{1,0},{2,6},{3,7},{4,5},{5,4},{6,2},{7,3},{8,9},{9,8},{10,14... | collective-permute-start | bytes 1572872 | tf_op jit(solution)/shard_map/ppermute | solution.py:30
  67.1 17.1 %collective-permute-start.12 = (bf16[128,2048]{1,0:T(8,128)(2,1)S(1)}, bf16[128,2048]{1,0:T(8,128)(2,1)S(1)}, u32[]{:S(2)}, u32[]{:S(2)}) collective-permute-start(bf16[128,2048]{1,0:T(8,128)(2,1)S(1)} %collective-permute-done.6.refs_7_), channel_id=1, source_target_pairs={{0,8},{1,9},{2,10},{3,11},{4,12},{5,13},{6,14},{7,15},{8,0},{9,1},... | collective-permute-start | bytes 1572872 | tf_op jit(solution)/shard_map/ppermute | solution.py:30
  122.7 22.9 %collective-permute-start.21 = (bf16[2,2,128,2048]{3,2,1,0:T(8,128)(2,1)S(1)}, bf16[2,2,128,2048]{3,2,1,0:T(8,128)(2,1)S(1)}, u32[]{:S(2)}, u32[]{:S(2)}) collective-permute-start(bf16[2,2,128,2048]{3,2,1,0:T(8,128)(2,1)S(1)} %get-tuple-element.47), channel_id=1, source_target_pairs={{0,2},{1,3},{2,0},{3,1},{4,6},{5,7},{6,4},{7,5},{8,10},{9,11},{10,... | collective-permute-start | bytes 6291464 | tf_op jit(solution)/shard_map/ppermute | solution.py:30
  130.7 14.9 %collective-permute-start.23 = (bf16[128,2048]{1,0:T(8,128)(2,1)S(1)}, bf16[128,2048]{1,0:T(8,128)(2,1)S(1)}, u32[]{:S(2)}, u32[]{:S(2)}) collective-permute-start(bf16[128,2048]{1,0:T(8,128)(2,1)S(1)} %get-tuple-element.53), channel_id=1, source_target_pairs={{0,8},{1,9},{2,10},{3,11},{4,12},{5,13},{6,14},{7,15},{8,0},{9,1},... | collective-permute-start | bytes 1572872 | tf_op jit(solution)/shard_map/ppermute | solution.py:30
  132.1 16.1 %collective-permute-start.27 = (bf16[128,2048]{1,0:T(8,128)(2,1)S(1)}, bf16[128,2048]{1,0:T(8,128)(2,1)S(1)}, u32[]{:S(2)}, u32[]{:S(2)}) collective-permute-start(bf16[128,2048]{1,0:T(8,128)(2,1)S(1)} %get-tuple-element.54), channel_id=1, source_target_pairs={{0,4},{1,5},{2,3},{3,2},{4,0},{5,1},{6,7},{7,6},{8,12},{9,13},{10,... | collective-permute-start | bytes 1572872 | tf_op jit(solution)/shard_map/ppermute | solution.py:30
  132.9 15.3 %collective-permute-start.26 = (bf16[128,2048]{1,0:T(8,128)(2,1)S(1)}, bf16[128,2048]{1,0:T(8,128)(2,1)S(1)}, u32[]{:S(2)}, u32[]{:S(2)}) collective-permute-start(bf16[128,2048]{1,0:T(8,128)(2,1)S(1)} %get-tuple-element.55), channel_id=1, source_target_pairs={{0,1},{1,0},{2,6},{3,7},{4,5},{5,4},{6,2},{7,3},{8,9},{9,8},{10,14... | collective-permute-start | bytes 1572872 | tf_op jit(solution)/shard_map/ppermute | solution.py:30
  146.7 17.0 %collective-permute-start.22 = (bf16[128,2048]{1,0:T(8,128)(2,1)S(1)}, bf16[128,2048]{1,0:T(8,128)(2,1)S(1)}, u32[]{:S(2)}, u32[]{:S(2)}) collective-permute-start(bf16[128,2048]{1,0:T(8,128)(2,1)S(1)} %fusion.16), channel_id=1, source_target_pairs={{0,1},{1,0},{2,6},{3,7},{4,5},{5,4},{6,2},{7,3},{8,9},{9,8},{10,14... | collective-permute-start | bytes 1572872 | tf_op jit(solution)/shard_map/ppermute | solution.py:30
  148.2 21.6 %collective-permute-start.20 = (bf16[2,2,128,2048]{3,2,1,0:T(8,128)(2,1)S(1)}, bf16[2,2,128,2048]{3,2,1,0:T(8,128)(2,1)S(1)}, u32[]{:S(2)}, u32[]{:S(2)}) collective-permute-start(bf16[2,2,128,2048]{3,2,1,0:T(8,128)(2,1)S(1)} %get-tuple-element.45), channel_id=1, source_target_pairs={{0,2},{1,3},{2,0},{3,1},{4,6},{5,7},{6,4},{7,5},{8,10},{9,11},{10,... | collective-permute-start | bytes 6291464 | tf_op jit(solution)/shard_map/ppermute | solution.py:30
  149.5 14.8 %collective-permute-start.28 = (bf16[128,2048]{1,0:T(8,128)(2,1)S(1)}, bf16[128,2048]{1,0:T(8,128)(2,1)S(1)}, u32[]{:S(2)}, u32[]{:S(2)}) collective-permute-start(bf16[128,2048]{1,0:T(8,128)(2,1)S(1)} %fusion.6), channel_id=1, source_target_pairs={{0,8},{1,9},{2,10},{3,11},{4,12},{5,13},{6,14},{7,15},{8,0},{9,1},... | collective-permute-start | bytes 1572872 | tf_op jit(solution)/shard_map/ppermute | solution.py:30
  157.8 23.3 %collective-permute-start.35 = (bf16[128,2048]{1,0:T(8,128)(2,1)S(1)}, bf16[128,2048]{1,0:T(8,128)(2,1)S(1)}, u32[]{:S(2)}, u32[]{:S(2)}) collective-permute-start(bf16[128,2048]{1,0:T(8,128)(2,1)S(1)} %get-tuple-element.57), channel_id=1, source_target_pairs={{0,8},{1,9},{2,10},{3,11},{4,12},{5,13},{6,14},{7,15},{8,0},{9,1},... | collective-permute-start | bytes 1572872 | tf_op jit(solution)/shard_map/ppermute | solution.py:30
  166.3 26.8 %collective-permute-start.29 = (bf16[128,2048]{1,0:T(8,128)(2,1)S(1)}, bf16[128,2048]{1,0:T(8,128)(2,1)S(1)}, u32[]{:S(2)}, u32[]{:S(2)}) collective-permute-start(bf16[128,2048]{1,0:T(8,128)(2,1)S(1)} %fusion.11), channel_id=1, source_target_pairs={{0,16},{1,17},{2,18},{3,19},{4,20},{5,21},{6,22},{7,23},{8,24},{9,... | collective-permute-start | bytes 1572872 | tf_op jit(solution)/shard_map/ppermute | solution.py:30
  168.0 15.6 %collective-permute-start.32 = (bf16[128,2048]{1,0:T(8,128)(2,1)S(1)}, bf16[128,2048]{1,0:T(8,128)(2,1)S(1)}, u32[]{:S(2)}, u32[]{:S(2)}) collective-permute-start(bf16[128,2048]{1,0:T(8,128)(2,1)S(1)} %get-tuple-element.50), channel_id=1, source_target_pairs={{0,4},{1,5},{2,3},{3,2},{4,0},{5,1},{6,7},{7,6},{8,12},{9,13},{10,... | collective-permute-start | bytes 1572872 | tf_op jit(solution)/shard_map/ppermute | solution.py:30
  169.2 14.3 %collective-permute-start.31 = (bf16[128,2048]{1,0:T(8,128)(2,1)S(1)}, bf16[128,2048]{1,0:T(8,128)(2,1)S(1)}, u32[]{:S(2)}, u32[]{:S(2)}) collective-permute-start(bf16[128,2048]{1,0:T(8,128)(2,1)S(1)} %get-tuple-element.56), channel_id=1, source_target_pairs={{0,1},{1,0},{2,6},{3,7},{4,5},{5,4},{6,2},{7,3},{8,9},{9,8},{10,14... | collective-permute-start | bytes 1572872 | tf_op jit(solution)/shard_map/ppermute | solution.py:30
  183.0 17.0 %collective-permute-start.34 = (bf16[128,2048]{1,0:T(8,128)(2,1)S(1)}, bf16[128,2048]{1,0:T(8,128)(2,1)S(1)}, u32[]{:S(2)}, u32[]{:S(2)}) collective-permute-start(bf16[128,2048]{1,0:T(8,128)(2,1)S(1)} %fusion.22), channel_id=1, source_target_pairs={{0,1},{1,0},{2,6},{3,7},{4,5},{5,4},{6,2},{7,3},{8,9},{9,8},{10,14... | collective-permute-start | bytes 1572872 | tf_op jit(solution)/shard_map/ppermute | solution.py:30
  183.9 18.6 %collective-permute-start.33 = (bf16[128,2048]{1,0:T(8,128)(2,1)S(1)}, bf16[128,2048]{1,0:T(8,128)(2,1)S(1)}, u32[]{:S(2)}, u32[]{:S(2)}) collective-permute-start(bf16[128,2048]{1,0:T(8,128)(2,1)S(1)} %fusion.4), channel_id=1, source_target_pairs={{0,8},{1,9},{2,10},{3,11},{4,12},{5,13},{6,14},{7,15},{8,0},{9,1},... | collective-permute-start | bytes 1572872 | tf_op jit(solution)/shard_map/ppermute | solution.py:30
  (19 other events, 177.3 us)
